TPU v7x, 256 devices: a whole 4x4x8 slice. The times are simulated.
256 devices in a mesh: blk: 16 (over x_hi, y, core), ab: 16 (over x_lo, z).
Axes of the slice: x: 4 (x_hi: 2, x_lo: 2; x = x_hi * 2 + x_lo), y: 4, z: 8, core: 2. Of those that a mesh axis runs over, the one named last changes fastest.
Arguments:
- amplitudes: bfloat16 [1024, 11264], P('blk'), may hold values from -6 to 6
- integrals: bfloat16 [32768, 11264], P(('blk', 'ab')), may hold values from -0.0546875 to 0.0546875
- live_rows: int32 [16], replicated, may hold values from 1 to 64, 640 in all
- partner: int32 [1024], replicated, may hold values from 0 to 1023, as said below
Outputs:
- ladder: float32 [1024, 32768], P(None, ('blk', 'ab'))
Inputs may be any that keep to these rules, and one draw needn't show every extreme that they name: `live_rows`: lengths of the blocks; the largest equals 64. An involution without fixed points: partner[partner[r]] = r and partner[r] != r.
All inputs are finite; a program needn't handle non-finite values.
Results may differ from a plain program's by a relative error of at most 0.0003.
Values may be sent and summed in bfloat16 or wider, within the bound.
No kernel may reach another device: no remote copies, remote signals or barrier semaphores. Data moves between devices by JAX's collectives and lax.ppermute only.
A program may use at most 128 MiB of HBM per device.

v0:
```python
import jax
import jax.numpy as jnp
from jax import lax
from jax.sharding import PartitionSpec as P


def passed_along(block, axis, distance):
    devices = range(lax.axis_size(axis))
    route = [((i - distance) % len(devices), i) for i in devices]
    return lax.ppermute(block, axis, route)


def block_product(rows, integrals):
    return lax.dot_general(
        rows, integrals, (((1,), (1,)), ((), ())), preferred_element_type=jnp.float32
    )


def shards(amplitudes, integrals, live_rows, partner):
    height = amplitudes.shape[0]
    count = lax.axis_size("blk")
    total = height * count
    partial_w = block_product(lax.all_gather(amplitudes, "blk", axis=0, tiled=True), integrals)
    slots = jnp.arange(total, dtype=jnp.int32)
    live = slots % height < jnp.repeat(live_rows, height, total_repeat_length=total)
    partial_w = jnp.where(live[:, None], partial_w, jnp.zeros_like(partial_w))
    mated = passed_along(partial_w, "ab", lax.axis_size("ab") // 2)
    return partial_w + mated[partner]


def solution(mesh):
    return jax.shard_map(
        shards,
        mesh=mesh,
        in_specs=(P("blk", None), P(("blk", "ab"), None), P(), P()),
        out_specs=P(None, ("blk", "ab")),
        check_vma=False,
    )
```

profile of v0, /device:TPU:1, one launch (start us, length us, event | category | flops | bytes accessed | tf_op | source)
XLA Modules:
  0.0 194.5 jit_solution(18076250899206524706)
XLA Ops:
  6.5 0.0 copy-start
  6.5 0.0 all-gather.2.cloned.1.call-start
  6.5 0.7 all-gather.2.cloned.1.call-update
  7.3 1.9 fusion.5
  9.2 0.8 add_add_fusion.1
  10.0 4.3 %compare_select_fusion.1 = (s32[1024,1]{0,1:T(1,128)S(1)}, s32[1024,1]{0,1:T(1,128)S(1)}) fusion(s32[]{:T(128)} %bitcast.13, s32[]{:T(128)} %bitcast.14, s32[]{:T(128)} %bitcast.15, s32[]{:T(128)} %bitcast.16, s32[]{:T(128)} %bitcast.17, s32[]{:T(128)} %bitcast.19, s32[]{:T(128)} %bitcast.18, s32[1024,1]{0,1:T(1,128)S(1)} %bitcast.30, s32[1024,1]{0,1:T(1,128)S(1)} %bitcast.29), kind=kLoop, calls=%fused_computation.12 | loop fusion | flops 14336 | bytes 16412 | tf_op jit(solution)/shard_map/jit(_take)/gather | solution.py:25
  14.3 0.1 compare_reduce_fusion.8
  14.4 6.4 %fusion = pred[1024]{0:T(1024)(128)(4,1)S(1)} fusion(pred[1024]{0:T(1024)(128)(4,1)S(1)} %get-tuple-element.25, pred[1024]{0:T(1024)(128)(4,1)S(1)} %get-tuple-element.24, pred[1024]{0:T(1024)(128)(4,1)S(1)} %get-tuple-element.23, pred[1024]{0:T(1024)(128)(4,1)S(1)} %get-tuple-element.22, pred[1024]{0:T(1024)(128)(4,1)S(1)} %get-tuple-element.21, ...), kind=kLoop, calls=%fused_computation.23 | loop fusion | flops 25600 | bytes 18500 | tf_op jit(solution)/shard_map/lt | solution.py:25
  20.8 0.0 copy-start.2
  20.8 136.7 %all-gather.2.cloned.1.call-done = bf16[1024,11264]{1,0:T(8,128)(2,1)} async-done(((bf16[64,11264]{1,0:T(8,128)(2,1)}), bf16[1024,11264]{1,0:T(8,128)(2,1)}) %all-gather.2.cloned.1.call-update) | async-done | bytes 23068688 | tf_op jit(solution)/shard_map/all_gather | solution.py:23
  157.5 0.0 copy-done
  157.5 10.7 %convolution_select_fusion = f32[1024,128]{1,0:T(8,128)S(1)} fusion(bf16[1024,11264]{1,0:T(8,128)(2,1)} %all-gather.2.cloned.1.call-done, bf16[128,11264]{1,0:T(8,128)(2,1)S(1)} %copy-done, pred[1024]{0:T(1024)(128)(4,1)S(1)} %fusion), kind=kOutput, calls=%fused_computation.1 | convolution fusion | flops 2952921088 | bytes 26477568 | tf_op jit(solution)/shard_map/dot_general | solution.py:14
  168.2 0.0 copy-start.1
  168.2 0.4 collective-permute-start
  168.6 0.4 copy-done.1
  169.0 0.0 copy-done.2
  169.0 12.6 %collective-permute-done = f32[1024,128]{1,0:T(8,128)S(1)} collective-permute-done((f32[1024,128]{1,0:T(8,128)S(1)}, f32[1024,128]{1,0:T(8,128)S(1)}, u32[]{:S(2)}, u32[]{:S(2)}) %collective-permute-start) | collective-permute-done | bytes 524320 | tf_op jit(solution)/shard_map/ppermute | solution.py:10
  181.6 4.0 %gather_fusion = f32[1024,128]{1,0:T(8,128)} fusion(f32[1024,128]{1,0:T(8,128)S(1)} %collective-permute-done, s32[1024]{0:T(1024)S(1)} %fusion.1), kind=kCustom, calls=%fused_computation | custom fusion | bytes 1052672 | tf_op jit(solution)/shard_map/gather | solution.py:28
  185.6 2.0 %add.80 = f32[1024,128]{1,0:T(8,128)} add(f32[1024,128]{1,0:T(8,128)} %copy-done.1, f32[1024,128]{1,0:T(8,128)} %gather_fusion) | non-fusion elementwise | flops 131072 | bytes 1572864 | tf_op jit(solution)/shard_map/add | solution.py:28
  (2 shorter events, 0.0 us)
Async XLA Ops:
  6.5 150.9 %copy-start = (bf16[128,11264]{1,0:T(8,128)(2,1)S(1)}, bf16[128,11264]{1,0:T(8,128)(2,1)}, u32[]{:S(2)}) copy-start(bf16[128,11264]{1,0:T(8,128)(2,1)} %param.7) | copy-start | bytes 8650756
  6.5 150.9 %all-gather.2.cloned.1.call-start = ((), (), s32[]{:S(2)}) async-start(), calls=%async_computation | async-start | bytes 24510464 | tf_op jit(solution)/shard_map/all_gather | solution.py:23
  20.8 148.2 %copy-start.2 = (s32[1024]{0:T(1024)S(1)}, s32[1024]{0:T(1024)}, u32[]{:S(2)}) copy-start(s32[1024]{0:T(1024)} %param.9) | copy-start | bytes 12292
  168.2 0.8 copy-start.1
  168.2 13.4 %collective-permute-start = (f32[1024,128]{1,0:T(8,128)S(1)}, f32[1024,128]{1,0:T(8,128)S(1)}, u32[]{:S(2)}, u32[]{:S(2)}) collective-permute-start(f32[1024,128]{1,0:T(8,128)S(1)} %convolution_select_fusion), channel_id=1, source_target_pairs={{8,0},{9,1},{10,2},{11,3},{12,4},{13,5},{14,6},{15,7},{0,8},{1,9},... | collective-permute-start | bytes 1572872 | tf_op jit(solution)/shard_map/ppermute | solution.py:10
Sparse Core Ops, SparseCore 0:
  10.1 147.2 all-gather.1
where the time goes:
time: 195 us; the launch traced here: 194 us
  waiting for transfers between devices  150 us (77%)
  other arithmetic  13.6 us (7%)
  between operations  13.4 us (7%)
  matrix products  10.7 us (5%)
  local copies, waits for them, and re-layouts  6.35 us (3%)
    all_gather x1, waiting for transfers between devices, shards(): lax.all_gather(amplitudes, 'blk', axis=0, tiled=True)  137 us
    ppermute x1, waiting for transfers between devices, passed_along(): return lax.ppermute(block, axis, route)  12.6 us
    dot_general x1, matrix products, block_product(): lax.dot_general(rows, integrals, (((1,), (1,)), ((), ())), preferred_elem...  10.7 us
    lt x1, other arithmetic, shards(): slots % height < jnp.repeat(live_rows, height, total_repeat_length=total)  6.36 us
    gather x2, other arithmetic, shards(): jnp.repeat(live_rows, height, total_repeat_length=total)  4.44 us
    gather x1, local copies, waits for them, and re-layouts, shards(): return partial_w + mated[partner]  3.99 us
  transfers between devices with their start and end apart: 2, of which 2 were waited for; matrix products, arithmetic and copies ran while one was open for 7% of the time, Pallas kernels for 0%

commit v1 on v0

v1 whole, which is shorter than its diff:
```python
import jax
import jax.numpy as jnp
from jax import lax
from jax.experimental import pallas as pl
from jax.experimental.pallas import tpu as pltpu
from jax.sharding import PartitionSpec as P

AXES = ("blk", "ab")
NX, NY, NZ = 4, 4, 8


def place(x, y, z, c):
    return ((((x // 2) * NY + y) * 2 + c) * 2 + x % 2) * NZ + z


def other(i, n, odd):
    return (i ^ 1) if not odd else ((((i + 1) % n) ^ 1) - 1) % n


MOVES = {
    "x0": lambda x, y, z, c: (other(x, NX, 0), y, z, c),
    "x1": lambda x, y, z, c: (other(x, NX, 1), y, z, c),
    "y0": lambda x, y, z, c: (x, other(y, NY, 0), z, c),
    "y1": lambda x, y, z, c: (x, other(y, NY, 1), z, c),
    "core": lambda x, y, z, c: (x, y, z, c ^ 1),
}


def swap(block, move):
    pairs = [
        (place(x, y, z, c), place(*MOVES[move](x, y, z, c)))
        for x in range(NX) for y in range(NY) for z in range(NZ) for c in range(2)
    ]
    return lax.ppermute(block, AXES, pairs)


def dot_t(a, b):
    return lax.dot_general(a, b, (((1,), (1,)), ((), ())), preferred_element_type=jnp.float32)


def halves(t):
    high = t.astype(jnp.bfloat16)
    return high, (t - high.astype(jnp.float32)).astype(jnp.bfloat16)


def dot(a, b):
    return jnp.dot(a, b, preferred_element_type=jnp.float32)


def symmetrize_kernel(slot_ref, mate_slot_ref, own_ref, mate_ref, mine_ref, sibling_ref):
    rows = mine_ref.shape[0]
    r = lax.broadcasted_iota(jnp.int32, (rows, 1), 0) + pl.program_id(0) * rows
    direct = (r == slot_ref[...]).astype(jnp.bfloat16)
    crossed = (r == mate_slot_ref[...]).astype(jnp.bfloat16)
    mh, ml = halves(mate_ref[...])
    oh, ol = halves(own_ref[...])
    out = (dot(direct, mh) + dot(crossed, oh)) + (dot(direct, ml) + dot(crossed, ol))
    width = mine_ref.shape[1]
    mine_ref[...] = out[:, :width]
    sibling_ref[...] = out[:, width:]


def symmetrize(slot, mate_slot, own, mate, total):
    n, w = own.shape
    rows = 256
    whole = lambda shape: pl.BlockSpec(shape, lambda i: (0, 0))
    return pl.pallas_call(
        symmetrize_kernel,
        grid=(total // rows,),
        in_specs=[whole((1, n)), whole((1, n)), whole((n, w)), whole((n, w))],
        out_specs=[pl.BlockSpec((rows, w // 2), lambda i: (i, 0))] * 2,
        out_shape=[jax.ShapeDtypeStruct((total, w // 2), jnp.float32)] * 2,
        compiler_params=pltpu.CompilerParams(vmem_limit_bytes=48 << 20),
        name="symmetrize",
    )(slot, mate_slot, own, mate)


def reorder_kernel(partner_ref, t_ref, o_ref):
    rows, n = o_ref.shape[0], t_ref.shape[0]
    pick = (partner_ref[...] == lax.broadcasted_iota(jnp.int32, (rows, n), 1)).astype(jnp.bfloat16)
    high, low = halves(t_ref[...])
    o_ref[...] = dot(pick, high) + dot(pick, low)


def reorder(partner, t):
    n, w = t.shape
    rows = 256
    return pl.pallas_call(
        reorder_kernel,
        grid=(n // rows,),
        in_specs=[pl.BlockSpec((rows, 1), lambda i: (i, 0)), pl.BlockSpec((n, w), lambda i: (0, 0))],
        out_specs=pl.BlockSpec((rows, w), lambda i: (i, 0)),
        out_shape=jax.ShapeDtypeStruct((n, w), jnp.float32),
        compiler_params=pltpu.CompilerParams(vmem_limit_bytes=48 << 20),
        name="reorder",
    )(partner[:, None], t)


def shards(amplitudes, integrals, live_rows, partner):
    height, depth = amplitudes.shape
    total = partner.shape[0]
    half = depth // 2
    blk, ab = lax.axis_index("blk"), lax.axis_index("ab")
    xh, y, c = blk // (2 * NY), (blk // 2) % NY, blk % 2
    xl = ab // NZ
    upper = (xh ^ xl) == 1
    keep = lambda t: jnp.where(upper, t[:, half:], t[:, :half])
    give = lambda t: jnp.where(upper, t[:, :half], t[:, half:])

    b_mine = keep(integrals)
    b_mate = swap(give(integrals), "x0")
    u = {"": keep(amplitudes)}
    u["a"] = swap(u[""], "x1")
    u["b"] = swap(u[""], "y0")
    u["c"] = swap(u[""], "y1")
    b_sib = swap(b_mine, "core")
    u["ab"] = swap(u["b"], "x1")
    u["bc"] = swap(u["c"], "y0")
    u["ac"] = swap(u["a"], "y1")
    cuts = [0, half * 15 // 44 // 128 * 128, half * 30 // 44 // 128 * 128, half]
    part = lambda t, i: t[:, cuts[i]:cuts[i + 1]]
    u["abc"] = jnp.concatenate(
        [swap(part(u["bc"], 0), "x1"), swap(part(u["ac"], 1), "y0"), swap(part(u["ab"], 2), "y1")], axis=1)
    b_mate_sib = swap(b_mate, "core")

    order = ["", "a", "b", "c", "ab", "bc", "ac", "abc"]
    groups = [order[:4], order[4:7], order[7:]]
    own, mate = [], []
    b_own = jnp.concatenate([b_mine, b_sib], axis=0)
    b_far = jnp.concatenate([b_mate, b_mate_sib], axis=0)
    for names in groups:
        rows = jnp.concatenate([u[n] for n in names], axis=0)
        own.append(dot_t(rows, b_own))
        mate.append(dot_t(rows, b_far))
    own, mate = jnp.concatenate(own, axis=0), jnp.concatenate(mate, axis=0)

    blocks = []
    for n in order:
        xh_n = xh ^ 1 if "a" in n else xh
        y_n = y
        if "b" in n:
            y_n = y_n ^ 1
        if "c" in n:
            y_n = (((y_n + 1) ^ 1) - 1) % NY
        blocks.append((xh_n * NY + y_n) * 2 + c)
    blocks = jnp.stack(blocks)
    lane = jnp.arange(height, dtype=jnp.int32)
    slot = (blocks[:, None] * height + lane[None, :]).reshape(-1)
    alive = (lane[None, :] < live_rows[blocks][:, None]).reshape(-1)
    mate_slot = jnp.where(alive, partner[slot], -1)[None, :]
    slot = jnp.where(alive, slot, -1)[None, :]

    mine, sibling = symmetrize(slot, mate_slot, own, mate, total)
    mine = mine + swap(sibling, "core")
    return swap(mine, "x0") + reorder(partner, mine)


def solution(mesh):
    return jax.shard_map(
        shards,
        mesh=mesh,
        in_specs=(P("blk", None), P(("blk", "ab"), None), P(), P()),
        out_specs=P(None, ("blk", "ab")),
        check_vma=False,
    )
```

time: 195 us -> 81.1 us (0.42)
  waiting for transfers between devices: 150 us -> 26.5 us
  starting transfers between devices: 0.38 us -> 24.1 us
  between operations: 13.4 us -> 0.28 us
  other arithmetic: 13.6 us -> 6.14 us
  Pallas kernels: 0 us -> 4.09 us
  matrix products: 10.7 us -> 13.6 us
    all_gather x1 -> x0, waiting for transfers between devices: 137 us -> none  [shards(): lax.all_gather(amplitudes, 'blk', axis=0, tiled=True)]
    ppermute x1 -> x14, starting transfers between devices: 0.38 us -> 24.1 us  [swap(): return lax.ppermute(block, AXES, pairs)]
    ppermute x1 -> x14, waiting for transfers between devices: 12.6 us -> 26.5 us  [swap(): return lax.ppermute(block, AXES, pairs)]
    lt x1, other arithmetic: 6.36 us -> 0.08 us  [shards(): alive = (lane[None, :] < live_rows[blocks][:, None]).reshape(-1)]
    select_n x0 -> x5, other arithmetic: none -> 4.99 us  [the longest x1 3.56 us: shards(): give = lambda t: jnp.where(upper, t[:, :half], t[:, half:])]
    gather x3 -> x1, other arithmetic: 4.45 us -> 0.01 us  [shards(): mate_slot = jnp.where(alive, partner[slot], -1)[None, :]]
    pallas_call x0 -> x2, Pallas kernels: none -> 4.09 us  [the longest x1 2.27 us: reorder(): pl.pallas_call(reorder_kernel, grid=(n // rows,), in_specs=[pl.BlockSpec(...]
    gather x2, local copies, waits for them, and re-layouts: 5.93 us -> 2.93 us  [the longest x1 2.29 us: shards(): mate_slot = jnp.where(alive, partner[slot], -1)[None, :]]
  transfers between devices with their start and end apart: 2 -> 14, of which waited for: 2 -> 4; matrix products, arithmetic and copies ran while one was open for 7% -> 23% of each run, Pallas kernels for 0% -> 3%
where the time goes in v1:
time: 81.1 us; the launch traced here: 80.7 us
  waiting for transfers between devices  26.5 us (33%)
  starting transfers between devices  24.1 us (30%)
  matrix products  13.6 us (17%)
  other arithmetic  6.14 us (8%)
  local copies, waits for them, and re-layouts  6.09 us (8%)
  Pallas kernels  4.09 us (5%)
    ppermute x14, waiting for transfers between devices, swap(): return lax.ppermute(block, AXES, pairs)  26.5 us
    ppermute x14, starting transfers between devices, swap(): return lax.ppermute(block, AXES, pairs)  24.1 us
    dot_general x6, matrix products, dot_t(): lax.dot_general(a, b, (((1,), (1,)), ((), ())), preferred_element_type=jn...  13.6 us
    select_n x1, other arithmetic, shards(): give = lambda t: jnp.where(upper, t[:, :half], t[:, half:])  3.56 us
    gather x1, local copies, waits for them, and re-layouts, shards(): mate_slot = jnp.where(alive, partner[slot], -1)[None, :]  2.29 us
    pallas_call x1, Pallas kernels, reorder(): pl.pallas_call(reorder_kernel, grid=(n // rows,), in_specs=[pl.BlockSpec(...  2.27 us
    pallas_call x1, Pallas kernels, symmetrize(): pl.pallas_call(symmetrize_kernel, grid=(total // rows,), in_specs=[whole(...  1.82 us
  transfers between devices with their start and end apart: 14, of which 4 were waited for; matrix products, arithmetic and copies ran while one was open for 23% of the time, Pallas kernels for 3%

profile of v1, /device:TPU:1, one launch (start us, length us, event | category | flops | bytes accessed | tf_op | source)
XLA Modules:
  0.0 80.7 jit_solution(2778529930943799634)
XLA Ops:
  0.0 1.4 %slice_select_fusion = bf16[64,5632]{1,0:T(8,128)(2,1)S(1)} fusion(bf16[64,11264]{1,0:T(8,128)(2,1)} %param.4, pred[]{:T(512)S(6)} %eq.10), kind=kLoop, calls=%fused_computation.9 | loop fusion | flops 360448 | bytes 2162689 | tf_op jit(solution)/shard_map/jit(_where)/select_n | solution.py:107
  1.4 2.2 %collective-permute-start.1 = (bf16[64,5632]{1,0:T(8,128)(2,1)S(1)}, bf16[64,5632]{1,0:T(8,128)(2,1)}, u32[]{:S(2)}, u32[]{:S(2)}) collective-permute-start(bf16[64,5632]{1,0:T(8,128)(2,1)S(1)} %slice_select_fusion), channel_id=1, source_target_pairs={{0,32},{16,48},{1,33},{17,49},{2,34},{18,50},{3,35},{19,51},{4,36}... | collective-permute-start | bytes 2162696 | tf_op jit(solution)/shard_map/ppermute | solution.py:34
  3.7 1.9 %collective-permute-start.2 = (bf16[64,5632]{1,0:T(8,128)(2,1)S(1)}, bf16[64,5632]{1,0:T(8,128)(2,1)}, u32[]{:S(2)}, u32[]{:S(2)}) collective-permute-start(bf16[64,5632]{1,0:T(8,128)(2,1)S(1)} %slice_select_fusion), channel_id=1, source_target_pairs={{0,96},{16,112},{1,97},{17,113},{2,98},{18,114},{3,99},{19,115},{4... | collective-permute-start | bytes 2162696 | tf_op jit(solution)/shard_map/ppermute | solution.py:34
  5.6 2.5 %collective-permute-start = (bf16[64,5632]{1,0:T(8,128)(2,1)S(1)}, bf16[64,5632]{1,0:T(8,128)(2,1)}, u32[]{:S(2)}, u32[]{:S(2)}) collective-permute-start(bf16[64,5632]{1,0:T(8,128)(2,1)S(1)} %slice_select_fusion), channel_id=1, source_target_pairs={{0,136},{16,152},{1,137},{17,153},{2,138},{18,154},{3,139},{19,155... | collective-permute-start | bytes 2162696 | tf_op jit(solution)/shard_map/ppermute | solution.py:34
  8.0 3.6 %broadcast_select_fusion = (bf16[128,5632]{1,0:T(8,128)(2,1)}, bf16[128,5632]{1,0:T(8,128)(2,1)}) fusion(pred[]{:T(512)S(6)} %eq.10, bf16[128,11264]{1,0:T(8,128)(2,1)} %param.5), kind=kLoop, calls=%fused_computation.4 | loop fusion | flops 1441792 | bytes 5767169 | tf_op jit(solution)/shard_map/jit(_where)/select_n | solution.py:108
  11.6 1.7 %collective-permute-start.3 = (bf16[128,5632]{1,0:T(8,128)(2,1)}, bf16[128,5632]{1,0:T(8,128)(2,1)}, u32[]{:S(2)}, u32[]{:S(2)}) collective-permute-start(bf16[128,5632]{1,0:T(8,128)(2,1)} %get-tuple-element.10), channel_id=1, source_target_pairs={{0,16},{16,0},{1,17},{17,1},{2,18},{18,2},{3,19},{19,3},{4,20},{20... | collective-permute-start | bytes 4325384 | tf_op jit(solution)/shard_map/ppermute | solution.py:34
  13.8 4.5 %collective-permute-done.1 = bf16[64,5632]{1,0:T(8,128)(2,1)} collective-permute-done((bf16[64,5632]{1,0:T(8,128)(2,1)S(1)}, bf16[64,5632]{1,0:T(8,128)(2,1)}, u32[]{:S(2)}, u32[]{:S(2)}) %collective-permute-start.1) | collective-permute-done | bytes 720928 | tf_op jit(solution)/shard_map/ppermute | solution.py:34
  18.3 3.7 %collective-permute-start.4 = (bf16[64,5632]{1,0:T(8,128)(2,1)}, bf16[64,5632]{1,0:T(8,128)(2,1)}, u32[]{:S(2)}, u32[]{:S(2)}) collective-permute-start(bf16[64,5632]{1,0:T(8,128)(2,1)} %collective-permute-done.1), channel_id=1, source_target_pairs={{0,136},{16,152},{1,137},{17,153},{2,138},{18,154},{3,139},{19,155... | collective-permute-start | bytes 2162696 | tf_op jit(solution)/shard_map/ppermute | solution.py:34
  22.0 1.3 %collective-permute-start.5 = (bf16[64,5632]{1,0:T(8,128)(2,1)}, bf16[64,5632]{1,0:T(8,128)(2,1)S(1)}, u32[]{:S(2)}, u32[]{:S(2)}) collective-permute-start(bf16[64,5632]{1,0:T(8,128)(2,1)} %collective-permute-done.2), channel_id=1, source_target_pairs={{0,32},{16,48},{1,33},{17,49},{2,34},{18,50},{3,35},{19,51},{4,36}... | collective-permute-start | bytes 2162696 | tf_op jit(solution)/shard_map/ppermute | solution.py:34
  23.3 1.9 %collective-permute-start.6 = (bf16[64,5632]{1,0:T(8,128)(2,1)}, bf16[64,5632]{1,0:T(8,128)(2,1)S(1)}, u32[]{:S(2)}, u32[]{:S(2)}) collective-permute-start(bf16[64,5632]{1,0:T(8,128)(2,1)} %collective-permute-done), channel_id=1, source_target_pairs={{0,96},{16,112},{1,97},{17,113},{2,98},{18,114},{3,99},{19,115},{4... | collective-permute-start | bytes 2162696 | tf_op jit(solution)/shard_map/ppermute | solution.py:34
  26.0 2.3 %gather_fusion.1 = s32[512]{0:T(512)S(1)} fusion(s32[1024]{0:T(1024)S(1)} %copy-done.1, s32[1024]{0:T(1024)S(1)} %get-tuple-element.13), kind=kCustom, calls=%fused_computation.1 | custom fusion | bytes 6144 | tf_op jit(solution)/shard_map/gather | solution.py:150
  28.3 9.8 %collective-permute-done.5 = bf16[64,5632]{1,0:T(8,128)(2,1)S(1)} collective-permute-done((bf16[64,5632]{1,0:T(8,128)(2,1)}, bf16[64,5632]{1,0:T(8,128)(2,1)S(1)}, u32[]{:S(2)}, u32[]{:S(2)}) %collective-permute-start.5) | collective-permute-done | bytes 720928 | tf_op jit(solution)/shard_map/ppermute | solution.py:34
  38.1 2.2 %collective-permute-start.7 = (bf16[64,1920]{1,0:T(8,128)(2,1)S(1)}, bf16[64,1920]{1,0:T(8,128)(2,1)S(1)}, u32[]{:S(2)}, u32[]{:S(2)}) collective-permute-start(bf16[64,1920]{1,0:T(8,128)(2,1)S(1)} %slice.34), channel_id=1, source_target_pairs={{0,136},{16,152},{1,137},{17,153},{2,138},{18,154},{3,139},{19,155... | collective-permute-start | bytes 737288 | tf_op jit(solution)/shard_map/ppermute | solution.py:34
  41.7 1.9 %collective-permute-start.9 = (bf16[64,1792]{1,0:T(8,128)(2,1)S(1)}, bf16[64,1792]{1,0:T(8,128)(2,1)S(1)}, u32[]{:S(2)}, u32[]{:S(2)}) collective-permute-start(bf16[64,1792]{1,0:T(8,128)(2,1)S(1)} %slice.36), channel_id=1, source_target_pairs={{0,96},{16,112},{1,97},{17,113},{2,98},{18,114},{3,99},{19,115},{4... | collective-permute-start | bytes 688136 | tf_op jit(solution)/shard_map/ppermute | solution.py:34
  43.6 1.2 %constant_dynamic-update-slice_fusion.2 = bf16[192,5632]{1,0:T(8,128)(2,1)S(1)} fusion(bf16[64,5632]{1,0:T(8,128)(2,1)} %collective-permute-done.4), kind=kLoop, calls=%fused_computation.15 | loop fusion | bytes 1441792
  44.8 3.4 %collective-permute-start.11 = (bf16[128,5632]{1,0:T(8,128)(2,1)S(1)}, bf16[128,5632]{1,0:T(8,128)(2,1)S(1)}, u32[]{:S(2)}, u32[]{:S(2)}) collective-permute-start(bf16[128,5632]{1,0:T(8,128)(2,1)S(1)} %collective-permute-done.10), channel_id=1, source_target_pairs={{0,16},{16,0},{1,17},{17,1},{2,18},{18,2},{3,19},{19,3},{4,20},{20... | collective-permute-start | bytes 4325384 | tf_op jit(solution)/shard_map/ppermute | solution.py:34
  48.4 3.4 %fusion.2 = f32[256,256]{1,0:T(8,128)S(1)} fusion(bf16[128,5632]{1,0:T(8,128)(2,1)} %collective-permute-done.3, bf16[128,5632]{1,0:T(8,128)(2,1)} %get-tuple-element.10, bf16[64,5632]{1,0:T(8,128)(2,1)} %collective-permute-done.2, bf16[64,5632]{1,0:T(8,128)(2,1)} %collective-permute-done.1, bf16[64,5632]{1,0:T(8,128)(2,1)} %collective-permute-done, ...), kind=kOutput, calls=%fused_computation.8 | convolution fusion | flops 755499008 | bytes 6029312 | tf_op jit(solution)/shard_map/dot_general | solution.py:38
  51.8 2.9 %fusion.1 = f32[192,256]{1,0:T(8,128)S(1)} fusion(bf16[192,5632]{1,0:T(8,128)(2,1)S(1)} %constant_dynamic-update-slice_fusion, bf16[128,5632]{1,0:T(8,128)(2,1)} %collective-permute-done.3, bf16[128,5632]{1,0:T(8,128)(2,1)} %get-tuple-element.10), kind=kOutput, calls=%fused_computation.7 | convolution fusion | flops 559415296 | bytes 5242880 | tf_op jit(solution)/shard_map/dot_general | solution.py:38
  54.8 2.8 %fusion = f32[64,256]{1,0:T(8,128)S(1)} fusion(bf16[64,5632]{1,0:T(8,128)(2,1)S(1)} %constant_dynamic-update-slice_fusion.3, bf16[128,5632]{1,0:T(8,128)(2,1)} %collective-permute-done.3, bf16[128,5632]{1,0:T(8,128)(2,1)} %get-tuple-element.10), kind=kOutput, calls=%fused_computation.6 | convolution fusion | flops 190316544 | bytes 3670016 | tf_op jit(solution)/shard_map/dot_general | solution.py:38
  59.8 2.5 %fusion.3 = f32[256,256]{1,0:T(8,128)S(1)} fusion(bf16[256,5632]{1,0:T(8,128)(2,1)S(1)} %constant_dynamic-update-slice_fusion.6, bf16[64,5632]{1,0:T(8,128)(2,1)} %collective-permute-done.2, bf16[64,5632]{1,0:T(8,128)(2,1)} %collective-permute-done.1, bf16[64,5632]{1,0:T(8,128)(2,1)} %collective-permute-done, bf16[64,5632]{1,0:T(8,128)(2,1)S(1)} %copy-done.3), kind=kOutput, calls=%fused_computation.12 | convolution fusion | flops 749731840 | bytes 6029312 | tf_op jit(solution)/shard_map/dot_general | solution.py:38
  62.3 1.8 %symmetrize.1 = (f32[1024,128]{1,0:T(8,128)S(1)}, f32[1024,128]{1,0:T(8,128)S(1)}) custom-call(s32[1,512]{1,0:T(1,128)S(1)} %get-tuple-element.12.slot_ref, s32[1,512]{1,0:T(1,128)S(1)} %get-tuple-element.11.mate_slot_ref, f32[512,256]{1,0:T(8,128)S(1)} %pad_maximum_fusion.5.own_ref, f32[512,256]{1,0:T(8,128)S(1)} %pad_maximum_fusion.6.mate_ref), custom_call_target="tpu_custom_call" | custom-call | tf_op jit(solution)/shard_map/symmetrize/pallas_call | solution.py:67
  65.0 1.5 %collective-permute-done.12 = f32[1024,128]{1,0:T(8,128)S(1)} collective-permute-done((f32[1024,128]{1,0:T(8,128)S(1)}, f32[1024,128]{1,0:T(8,128)S(1)}, u32[]{:S(2)}, u32[]{:S(2)}) %collective-permute-start.12) | collective-permute-done | bytes 524320 | tf_op jit(solution)/shard_map/ppermute | solution.py:34
  66.9 2.3 %reorder.1 = f32[1024,128]{1,0:T(8,128)S(1)} custom-call(s32[1024,1]{1,0:T(8,128)S(1)} %copy.5.partner_ref, f32[1024,128]{1,0:T(8,128)S(1)} %add.166.t_ref), custom_call_target="tpu_custom_call" | custom-call | tf_op jit(solution)/shard_map/reorder/pallas_call | solution.py:88
  69.2 10.6 %collective-permute-done.13 = f32[1024,128]{1,0:T(8,128)S(1)} collective-permute-done((f32[1024,128]{1,0:T(8,128)S(1)}, f32[1024,128]{1,0:T(8,128)S(1)}, u32[]{:S(2)}, u32[]{:S(2)}) %collective-permute-start.13) | collective-permute-done | bytes 524320 | tf_op jit(solution)/shard_map/ppermute | solution.py:34
  (52 shorter events, 7.2 us)
Async XLA Ops:
  0.0 25.2 %copy-start = (s32[16]{0:T(128)S(1)}, s32[16]{0:T(128)}, u32[]{:S(2)}) copy-start(s32[16]{0:T(128)} %param.6) | copy-start | bytes 196
  1.4 10.2 %copy-start.2 = (bf16[64,5632]{1,0:T(8,128)(2,1)}, bf16[64,5632]{1,0:T(8,128)(2,1)S(1)}, u32[]{:S(2)}) copy-start(bf16[64,5632]{1,0:T(8,128)(2,1)S(1)} %slice_select_fusion) | copy-start | bytes 2162692
  1.4 24.6 %copy-start.1 = (s32[1024]{0:T(1024)S(1)}, s32[1024]{0:T(1024)}, u32[]{:S(2)}) copy-start(s32[1024]{0:T(1024)} %param.7) | copy-start | bytes 12292
  1.4 16.8 %collective-permute-start.1 = (bf16[64,5632]{1,0:T(8,128)(2,1)S(1)}, bf16[64,5632]{1,0:T(8,128)(2,1)}, u32[]{:S(2)}, u32[]{:S(2)}) collective-permute-start(bf16[64,5632]{1,0:T(8,128)(2,1)S(1)} %slice_select_fusion), channel_id=1, source_target_pairs={{0,32},{16,48},{1,33},{17,49},{2,34},{18,50},{3,35},{19,51},{4,36}... | collective-permute-start | bytes 2162696 | tf_op jit(solution)/shard_map/ppermute | solution.py:34
  3.7 18.3 %collective-permute-start.2 = (bf16[64,5632]{1,0:T(8,128)(2,1)S(1)}, bf16[64,5632]{1,0:T(8,128)(2,1)}, u32[]{:S(2)}, u32[]{:S(2)}) collective-permute-start(bf16[64,5632]{1,0:T(8,128)(2,1)S(1)} %slice_select_fusion), channel_id=1, source_target_pairs={{0,96},{16,112},{1,97},{17,113},{2,98},{18,114},{3,99},{19,115},{4... | collective-permute-start | bytes 2162696 | tf_op jit(solution)/shard_map/ppermute | solution.py:34
  5.6 17.7 %collective-permute-start = (bf16[64,5632]{1,0:T(8,128)(2,1)S(1)}, bf16[64,5632]{1,0:T(8,128)(2,1)}, u32[]{:S(2)}, u32[]{:S(2)}) collective-permute-start(bf16[64,5632]{1,0:T(8,128)(2,1)S(1)} %slice_select_fusion), channel_id=1, source_target_pairs={{0,136},{16,152},{1,137},{17,153},{2,138},{18,154},{3,139},{19,155... | collective-permute-start | bytes 2162696 | tf_op jit(solution)/shard_map/ppermute | solution.py:34
  11.6 33.2 %collective-permute-start.10 = (bf16[128,5632]{1,0:T(8,128)(2,1)}, bf16[128,5632]{1,0:T(8,128)(2,1)S(1)}, u32[]{:S(2)}, u32[]{:S(2)}) collective-permute-start(bf16[128,5632]{1,0:T(8,128)(2,1)} %get-tuple-element.9), channel_id=1, source_target_pairs={{0,8},{16,24},{1,9},{17,25},{2,10},{18,26},{3,11},{19,27},{4,12},{... | collective-permute-start | bytes 4325384 | tf_op jit(solution)/shard_map/ppermute | solution.py:34
  11.6 36.8 %collective-permute-start.3 = (bf16[128,5632]{1,0:T(8,128)(2,1)}, bf16[128,5632]{1,0:T(8,128)(2,1)}, u32[]{:S(2)}, u32[]{:S(2)}) collective-permute-start(bf16[128,5632]{1,0:T(8,128)(2,1)} %get-tuple-element.10), channel_id=1, source_target_pairs={{0,16},{16,0},{1,17},{17,1},{2,18},{18,2},{3,19},{19,3},{4,20},{20... | collective-permute-start | bytes 4325384 | tf_op jit(solution)/shard_map/ppermute | solution.py:34
  18.3 22.5 %collective-permute-start.4 = (bf16[64,5632]{1,0:T(8,128)(2,1)}, bf16[64,5632]{1,0:T(8,128)(2,1)}, u32[]{:S(2)}, u32[]{:S(2)}) collective-permute-start(bf16[64,5632]{1,0:T(8,128)(2,1)} %collective-permute-done.1), channel_id=1, source_target_pairs={{0,136},{16,152},{1,137},{17,153},{2,138},{18,154},{3,139},{19,155... | collective-permute-start | bytes 2162696 | tf_op jit(solution)/shard_map/ppermute | solution.py:34
  22.0 16.1 %collective-permute-start.5 = (bf16[64,5632]{1,0:T(8,128)(2,1)}, bf16[64,5632]{1,0:T(8,128)(2,1)S(1)}, u32[]{:S(2)}, u32[]{:S(2)}) collective-permute-start(bf16[64,5632]{1,0:T(8,128)(2,1)} %collective-permute-done.2), channel_id=1, source_target_pairs={{0,32},{16,48},{1,33},{17,49},{2,34},{18,50},{3,35},{19,51},{4,36}... | collective-permute-start | bytes 2162696 | tf_op jit(solution)/shard_map/ppermute | solution.py:34
  23.3 17.1 %collective-permute-start.6 = (bf16[64,5632]{1,0:T(8,128)(2,1)}, bf16[64,5632]{1,0:T(8,128)(2,1)S(1)}, u32[]{:S(2)}, u32[]{:S(2)}) collective-permute-start(bf16[64,5632]{1,0:T(8,128)(2,1)} %collective-permute-done), channel_id=1, source_target_pairs={{0,96},{16,112},{1,97},{17,113},{2,98},{18,114},{3,99},{19,115},{4... | collective-permute-start | bytes 2162696 | tf_op jit(solution)/shard_map/ppermute | solution.py:34
  38.1 16.6 %collective-permute-start.7 = (bf16[64,1920]{1,0:T(8,128)(2,1)S(1)}, bf16[64,1920]{1,0:T(8,128)(2,1)S(1)}, u32[]{:S(2)}, u32[]{:S(2)}) collective-permute-start(bf16[64,1920]{1,0:T(8,128)(2,1)S(1)} %slice.34), channel_id=1, source_target_pairs={{0,136},{16,152},{1,137},{17,153},{2,138},{18,154},{3,139},{19,155... | collective-permute-start | bytes 737288 | tf_op jit(solution)/shard_map/ppermute | solution.py:34
  40.4 14.4 %collective-permute-start.8 = (bf16[64,1920]{1,0:T(8,128)(2,1)S(1)}, bf16[64,1920]{1,0:T(8,128)(2,1)S(1)}, u32[]{:S(2)}, u32[]{:S(2)}) collective-permute-start(bf16[64,1920]{1,0:T(8,128)(2,1)S(1)} %slice.35), channel_id=1, source_target_pairs={{0,32},{16,48},{1,33},{17,49},{2,34},{18,50},{3,35},{19,51},{4,36}... | collective-permute-start | bytes 737288 | tf_op jit(solution)/shard_map/ppermute | solution.py:34
  41.7 13.1 %collective-permute-start.9 = (bf16[64,1792]{1,0:T(8,128)(2,1)S(1)}, bf16[64,1792]{1,0:T(8,128)(2,1)S(1)}, u32[]{:S(2)}, u32[]{:S(2)}) collective-permute-start(bf16[64,1792]{1,0:T(8,128)(2,1)S(1)} %slice.36), channel_id=1, source_target_pairs={{0,96},{16,112},{1,97},{17,113},{2,98},{18,114},{3,99},{19,115},{4... | collective-permute-start | bytes 688136 | tf_op jit(solution)/shard_map/ppermute | solution.py:34
  44.8 3.6 %copy-start.3 = (bf16[64,5632]{1,0:T(8,128)(2,1)S(1)}, bf16[64,5632]{1,0:T(8,128)(2,1)}, u32[]{:S(2)}) copy-start(bf16[64,5632]{1,0:T(8,128)(2,1)} %copy-done.2) | copy-start | bytes 2162692
  44.8 12.9 %collective-permute-start.11 = (bf16[128,5632]{1,0:T(8,128)(2,1)S(1)}, bf16[128,5632]{1,0:T(8,128)(2,1)S(1)}, u32[]{:S(2)}, u32[]{:S(2)}) collective-permute-start(bf16[128,5632]{1,0:T(8,128)(2,1)S(1)} %collective-permute-done.10), channel_id=1, source_target_pairs={{0,16},{16,0},{1,17},{17,1},{2,18},{18,2},{3,19},{19,3},{4,20},{20... | collective-permute-start | bytes 4325384 | tf_op jit(solution)/shard_map/ppermute | solution.py:34
  64.2 2.4 %collective-permute-start.12 = (f32[1024,128]{1,0:T(8,128)S(1)}, f32[1024,128]{1,0:T(8,128)S(1)}, u32[]{:S(2)}, u32[]{:S(2)}) collective-permute-start(f32[1024,128]{1,0:T(8,128)S(1)} %get-tuple-element.8), channel_id=1, source_target_pairs={{0,16},{16,0},{1,17},{17,1},{2,18},{18,2},{3,19},{19,3},{4,20},{20... | collective-permute-start | bytes 1572872 | tf_op jit(solution)/shard_map/ppermute | solution.py:34
  66.6 13.2 %collective-permute-start.13 = (f32[1024,128]{1,0:T(8,128)S(1)}, f32[1024,128]{1,0:T(8,128)S(1)}, u32[]{:S(2)}, u32[]{:S(2)}) collective-permute-start(f32[1024,128]{1,0:T(8,128)S(1)} %add.166.t_ref), channel_id=1, source_target_pairs={{0,8},{16,24},{1,9},{17,25},{2,10},{18,26},{3,11},{19,27},{4,12},{... | collective-permute-start | bytes 1572872 | tf_op jit(solution)/shard_map/ppermute | solution.py:34

commit v2 on v0

v2 whole, which is shorter than its diff:
```python
import jax
import jax.numpy as jnp
from jax import lax
from jax.experimental import pallas as pl
from jax.experimental.pallas import tpu as pltpu
from jax.sharding import PartitionSpec as P

AXES = ("blk", "ab")
NX, NY, NZ = 4, 4, 8
ROOM = pltpu.CompilerParams(vmem_limit_bytes=16 << 20)
ANYWHERE = pl.BlockSpec(memory_space=pl.ANY)
WHOLE = pl.BlockSpec(memory_space=pltpu.VMEM)


def place(x, y, z, c):
    return ((((x // 2) * NY + y) * 2 + c) * 2 + x % 2) * NZ + z


def other(i, n, odd):
    return ((((i + 1) % n) ^ 1) - 1) % n if odd else i ^ 1


MOVES = {
    "x0": lambda x, y, z, c: (other(x, NX, 0), y, z, c),
    "x1": lambda x, y, z, c: (other(x, NX, 1), y, z, c),
    "y0": lambda x, y, z, c: (x, other(y, NY, 0), z, c),
    "y1": lambda x, y, z, c: (x, other(y, NY, 1), z, c),
    "core": lambda x, y, z, c: (x, y, z, c ^ 1),
}


def swap(block, move):
    pairs = [
        (place(x, y, z, c), place(*MOVES[move](x, y, z, c)))
        for x in range(NX) for y in range(NY) for z in range(NZ) for c in range(2)
    ]
    return lax.ppermute(block, AXES, pairs)


def dot_t(a, b):
    return lax.dot_general(a, b, (((1,), (1,)), ((), ())), preferred_element_type=jnp.float32)


def dot(a, b):
    return jnp.dot(a, b, preferred_element_type=jnp.float32)


def halves(t):
    high = t.astype(jnp.bfloat16)
    return high, (t - high.astype(jnp.float32)).astype(jnp.bfloat16)


def cost(us):
    return pl.CostEstimate(flops=int(us * 1e9), bytes_accessed=int(us * 3e6), transcendentals=0)


def tied(value, *before):
    return lax.optimization_barrier((value, *before))[0]


def columns(ref, which, width):
    return ref.at[:, pl.ds(pl.multiple_of(which * width, width), width)]


def split_kernel(which_ref, a_ref, b_ref, keep_ref, give_ref, sem):
    width = keep_ref.shape[1]
    which = which_ref[0]
    keep = pltpu.make_async_copy(columns(a_ref, which, width), keep_ref, sem.at[0])
    give = pltpu.make_async_copy(columns(b_ref, 1 - which, width), give_ref, sem.at[1])
    keep.start()
    give.start()
    keep.wait()
    give.wait()


def split(which, a, b):
    half = a.shape[1] // 2
    return pl.pallas_call(
        split_kernel,
        in_specs=[pl.BlockSpec(memory_space=pltpu.SMEM), ANYWHERE, ANYWHERE],
        out_specs=[WHOLE, WHOLE],
        out_shape=[jax.ShapeDtypeStruct((t.shape[0], half), t.dtype) for t in (a, b)],
        scratch_shapes=[pltpu.SemaphoreType.DMA((2,))],
        cost_estimate=cost(2),
        name="split",
    )(which, a, b)


def first_kernel(n, which_ref, mine_ref, sibling_ref, *refs):
    rows, t_ref, cols_ref, held_ref, sem = refs[:n], *refs[n:]
    width = cols_ref.shape[1]
    high = mine_ref.shape[0]
    low = rows[0].shape[0]
    copies = [
        pltpu.make_async_copy(columns(mine_ref, which_ref[0], width), cols_ref.at[pl.ds(0, high)], sem.at[n]),
        pltpu.make_async_copy(columns(sibling_ref, which_ref[0], width), cols_ref.at[pl.ds(high, high)], sem.at[n + 1]),
    ] + [pltpu.make_async_copy(r, held_ref.at[pl.ds(i * low, low)], sem.at[i]) for i, r in enumerate(rows)]
    for copy in copies:
        copy.start()
    for copy in copies:
        copy.wait()
    t_ref[...] = dot_t(held_ref[...], cols_ref[...])


def first_product(which, mine, sibling, rows):
    n, high = len(rows), mine.shape[0]
    low, width = rows[0].shape
    return pl.pallas_call(
        lambda *refs: first_kernel(n, *refs),
        in_specs=[pl.BlockSpec(memory_space=pltpu.SMEM)] + [ANYWHERE] * (2 + n),
        out_specs=[WHOLE] * 3,
        out_shape=[
            jax.ShapeDtypeStruct((n * low, 2 * high), jnp.float32),
            jax.ShapeDtypeStruct((2 * high, width), mine.dtype),
            jax.ShapeDtypeStruct((n * low, width), mine.dtype),
        ],
        scratch_shapes=[pltpu.SemaphoreType.DMA((n + 2,))],
        compiler_params=ROOM,
        cost_estimate=cost(3),
        name="first_product",
    )(which, mine, sibling, *rows)


def pack_kernel(n, *refs):
    rows, out_ref, sem = refs[:n], *refs[n:]
    low = rows[0].shape[0]
    copies = [pltpu.make_async_copy(r, out_ref.at[pl.ds(i * low, low)], sem.at[i]) for i, r in enumerate(rows)]
    for copy in copies:
        copy.start()
    for copy in copies:
        copy.wait()


def pack(rows):
    n = len(rows)
    low, width = rows[0].shape
    return pl.pallas_call(
        lambda *refs: pack_kernel(n, *refs),
        in_specs=[ANYWHERE] * n,
        out_specs=WHOLE,
        out_shape=jax.ShapeDtypeStruct((n * low, width), rows[0].dtype),
        scratch_shapes=[pltpu.SemaphoreType.DMA((n,))],
        compiler_params=ROOM,
        cost_estimate=cost(2),
        name="pack",
    )(*rows)


def spread(slot_ref, partner_ref):
    r = lax.broadcasted_iota(jnp.int32, partner_ref.shape, 0)
    direct = (r == slot_ref[...]).astype(jnp.bfloat16)
    crossed = (partner_ref[...] == slot_ref[...]).astype(jnp.bfloat16)
    return direct, crossed


def symmetrize_kernel(n, slot_ref, partner_ref, *refs):
    own = jnp.concatenate([r[...] for r in refs[:n]], axis=0)
    mate = jnp.concatenate([r[...] for r in refs[n:2 * n]], axis=0)
    mine_ref, sibling_ref, largest_ref = refs[2 * n:]
    direct, crossed = spread(slot_ref, partner_ref)
    mh, ml = halves(mate)
    oh, ol = halves(own)
    out = (dot(direct, mh) + dot(crossed, oh)) + (dot(direct, ml) + dot(crossed, ol))
    total, width = mine_ref.shape
    mine, sibling = out[:, :width], out[:, width:]
    mine_ref[...] = mine
    sibling_ref[:total] = sibling
    largest_ref[...] = jnp.full(largest_ref.shape, jnp.max(jnp.abs(mine)))
    sibling_ref[total:] = jnp.full(largest_ref.shape, jnp.max(jnp.abs(sibling)))


def symmetrize(slot, partner, own, mate):
    total, width = partner.shape[0], own[0].shape[1] // 2
    return pl.pallas_call(
        lambda *refs: symmetrize_kernel(len(own), *refs),
        out_shape=[jax.ShapeDtypeStruct((n, width), jnp.float32) for n in (total, total + 8, 8)],
        compiler_params=ROOM,
        cost_estimate=cost(2),
        name="symmetrize",
    )(slot, partner, *own, *mate)


def reorder_kernel(partner_ref, t_ref, o_ref):
    n = t_ref.shape[0]
    pick = (partner_ref[...] == lax.broadcasted_iota(jnp.int32, (n, n), 1)).astype(jnp.bfloat16)
    high, low = halves(t_ref[...])
    o_ref[...] = dot(pick, high) + dot(pick, low)


def reorder(partner, t):
    return pl.pallas_call(
        reorder_kernel,
        out_shape=jax.ShapeDtypeStruct(t.shape, jnp.float32),
        compiler_params=ROOM,
        cost_estimate=cost(2),
        name="reorder",
    )(partner, t)


def shards(amplitudes, integrals, live_rows, partner):
    height, depth = amplitudes.shape
    total = partner.shape[0]
    half = depth // 2
    blk, ab = lax.axis_index("blk"), lax.axis_index("ab")
    xh, y, c = blk // (2 * NY), (blk // 2) % NY, blk % 2
    which = (xh ^ (ab // NZ)).astype(jnp.int32)[None]
    partner = partner[:, None]

    names = ["", "a", "b", "c", "ab", "bc", "ac", "abc"]
    blocks = []
    for n in names:
        xh_n, y_n = (xh ^ 1 if "a" in n else xh), y
        if "b" in n:
            y_n = y_n ^ 1
        if "c" in n:
            y_n = (((y_n + 1) ^ 1) - 1) % NY
        blocks.append((xh_n * NY + y_n) * 2 + c)
    blocks = jnp.stack(blocks)
    lane = jnp.arange(height, dtype=jnp.int32)
    alive = lane[None, :] < live_rows[blocks][:, None]
    slot = jnp.where(alive, blocks[:, None] * height + lane[None, :], -1).reshape(1, -1)

    u = {}
    u[""], given = split(which, amplitudes, integrals)
    u["a"] = swap(u[""], "x1")
    u["b"] = swap(u[""], "y0")
    u["c"] = swap(u[""], "y1")
    b_mate = swap(given, "x0")
    b_sib = swap(integrals, "core")
    u["ab"] = swap(u["b"], "x1")
    u["bc"] = swap(u["c"], "y0")
    u["ac"] = swap(u["a"], "y1")
    rows = [u[n] for n in names[:7]]
    which, slot, partner = lax.optimization_barrier((which, slot, partner))
    own_first, b_own, first = first_product(which, integrals, b_sib, rows[:4])
    cuts = [0, half * 15 // 44 // 128 * 128, half * 30 // 44 // 128 * 128, half]
    cut = [u[n][:, cuts[i]:cuts[i + 1]] for i, n in enumerate(("bc", "ac", "ab"))]
    last = jnp.concatenate([swap(t, move) for t, move in zip(cut, ("x1", "y0", "y1"))], axis=1)
    b_mate = tied(b_mate, *cut)
    b_mate_sib = swap(b_mate, "core")
    second = pack(rows[4:])
    own = [own_first, dot_t(second, b_own), dot_t(last, b_own)]
    b_far = jnp.concatenate([b_mate, b_mate_sib], axis=0)
    mate = [dot_t(t, b_far) for t in (first, second, last)]
    mine, sibling, largest = symmetrize(slot, partner, own, mate)
    sibling = swap(sibling, "core")
    mine = mine + sibling[:total]
    bound = largest[:1] + sibling[total:total + 1]
    power = jnp.clip(14.0 - jnp.ceil(jnp.log2(jnp.maximum(bound, 1e-37))), -120.0, 120.0)
    sent = jnp.concatenate(
        [(mine * jnp.exp2(power)).astype(jnp.float16), jnp.broadcast_to(power.astype(jnp.float16), (16, mine.shape[1]))],
        axis=0)
    came = swap(sent, "x0")
    scale = jnp.exp2(-came[total:total + 1].astype(jnp.float32))
    return came[:total].astype(jnp.float32) * scale + reorder(partner, mine)


def solution(mesh):
    return jax.shard_map(
        shards,
        mesh=mesh,
        in_specs=(P("blk", None), P(("blk", "ab"), None), P(), P()),
        out_specs=P(None, ("blk", "ab")),
        check_vma=False,
    )
```

time: 195 us -> 73.4 us (0.38)
  waiting for transfers between devices: 150 us -> 28.5 us
  starting transfers between devices: 0.38 us -> 25.6 us
  between operations: 13.4 us -> 0.22 us
  other arithmetic: 13.6 us -> 1.16 us
  Pallas kernels: 0 us -> 9.95 us
  matrix products: 10.7 us -> 5.05 us
  local copies, waits for them, and re-layouts: 6.35 us -> 2.82 us
    all_gather x1 -> x0, waiting for transfers between devices: 137 us -> none  [shards(): lax.all_gather(amplitudes, 'blk', axis=0, tiled=True)]
    ppermute x1 -> x14, starting transfers between devices: 0.38 us -> 25.6 us  [swap(): return lax.ppermute(block, AXES, pairs)]
    ppermute x1 -> x14, waiting for transfers between devices: 12.6 us -> 28.5 us  [swap(): return lax.ppermute(block, AXES, pairs)]
    pallas_call x0 -> x5, Pallas kernels: none -> 9.95 us  [the longest x1 3.33 us: first_product(): pl.pallas_call(lambda *refs: first_kernel(n, *refs), in_specs=[pl.BlockSp...]
    lt x1 -> x0, other arithmetic: 6.36 us -> none  [shards(): slots % height < jnp.repeat(live_rows, height, total_repeat_length=total)]
    dot_general x1 -> x5, matrix products: 10.7 us -> 5.05 us  [dot_t(): lax.dot_general(a, b, (((1,), (1,)), ((), ())), preferred_element_type=jn...]
    gather x2 -> x1, local copies, waits for them, and re-layouts: 5.93 us -> 0.64 us  [shards(): alive = lane[None, :] < live_rows[blocks][:, None]]
    gather x3 -> x1, other arithmetic: 4.45 us -> 0.01 us  [shards(): alive = lane[None, :] < live_rows[blocks][:, None]]
  transfers between devices with their start and end apart: 2 -> 14, of which waited for: 2 -> 4; matrix products, arithmetic and copies ran while one was open for 7% -> 7% of each run, Pallas kernels for 0% -> 8%
where the time goes in v2:
time: 73.4 us; the launch traced here: 73.2 us
  waiting for transfers between devices  28.5 us (39%)
  starting transfers between devices  25.6 us (35%)
  Pallas kernels  9.95 us (14%)
  matrix products  5.05 us (7%)
  local copies, waits for them, and re-layouts  2.82 us (4%)
  other arithmetic  1.16 us (2%)
    ppermute x14, waiting for transfers between devices, swap(): return lax.ppermute(block, AXES, pairs)  28.5 us
    ppermute x14, starting transfers between devices, swap(): return lax.ppermute(block, AXES, pairs)  25.6 us
    dot_general x5, matrix products, dot_t(): lax.dot_general(a, b, (((1,), (1,)), ((), ())), preferred_element_type=jn...  5.05 us
    pallas_call x1, Pallas kernels, first_product(): pl.pallas_call(lambda *refs: first_kernel(n, *refs), in_specs=[pl.BlockSp...  3.33 us
    pallas_call x1, Pallas kernels, split(): pl.pallas_call(split_kernel, in_specs=[pl.BlockSpec(memory_space=pltpu.SM...  3.01 us
    unnamed x9, local copies, waits for them, and re-layouts  1.51 us
  transfers between devices with their start and end apart: 14, of which 4 were waited for; matrix products, arithmetic and copies ran while one was open for 7% of the time, Pallas kernels for 8%

profile of v2, /device:TPU:1, one launch (start us, length us, event | category | flops | bytes accessed | tf_op | source)
XLA Modules:
  0.0 73.2 jit_solution(12477777498056821716)
XLA Ops:
  0.0 3.0 %split.1 = (bf16[64,5632]{1,0:T(8,128)(2,1)}, bf16[128,5632]{1,0:T(8,128)(2,1)}) custom-call(s32[1]{0:T(128)} %bitcast.which_ref.refs_0_, bf16[64,11264]{1,0:T(8,128)(2,1)} %a_ref.1, bf16[128,11264]{1,0:T(8,128)(2,1)} %refs_1_.1), custom_call_target="tpu_custom_call" | custom-call | flops 2000000000 | bytes 6000000 | tf_op jit(solution)/shard_map/split/pallas_call | solution.py:78
  3.0 2.2 %collective-permute-start.2 = (bf16[64,5632]{1,0:T(8,128)(2,1)}, bf16[64,5632]{1,0:T(8,128)(2,1)S(1)}, u32[]{:S(2)}, u32[]{:S(2)}) collective-permute-start(bf16[64,5632]{1,0:T(8,128)(2,1)} %get-tuple-element.20.refs_3_), channel_id=1, source_target_pairs={{0,32},{16,48},{1,33},{17,49},{2,34},{18,50},{3,35},{19,51},{4,36}... | collective-permute-start | bytes 2162696 | tf_op jit(solution)/shard_map/ppermute | solution.py:37
  5.2 1.9 %collective-permute-start.3 = (bf16[64,5632]{1,0:T(8,128)(2,1)}, bf16[64,5632]{1,0:T(8,128)(2,1)}, u32[]{:S(2)}, u32[]{:S(2)}) collective-permute-start(bf16[64,5632]{1,0:T(8,128)(2,1)} %get-tuple-element.20.refs_3_), channel_id=1, source_target_pairs={{0,96},{16,112},{1,97},{17,113},{2,98},{18,114},{3,99},{19,115},{4... | collective-permute-start | bytes 2162696 | tf_op jit(solution)/shard_map/ppermute | solution.py:37
  7.1 2.5 %collective-permute-start.1 = (bf16[64,5632]{1,0:T(8,128)(2,1)}, bf16[64,5632]{1,0:T(8,128)(2,1)}, u32[]{:S(2)}, u32[]{:S(2)}) collective-permute-start(bf16[64,5632]{1,0:T(8,128)(2,1)} %get-tuple-element.20.refs_3_), channel_id=1, source_target_pairs={{0,136},{16,152},{1,137},{17,153},{2,138},{18,154},{3,139},{19,155... | collective-permute-start | bytes 2162696 | tf_op jit(solution)/shard_map/ppermute | solution.py:37
  9.6 1.7 %collective-permute-start = (bf16[128,11264]{1,0:T(8,128)(2,1)}, bf16[128,11264]{1,0:T(8,128)(2,1)}, u32[]{:S(2)}, u32[]{:S(2)}) collective-permute-start(bf16[128,11264]{1,0:T(8,128)(2,1)} %refs_1_.1), channel_id=1, source_target_pairs={{0,16},{16,0},{1,17},{17,1},{2,18},{18,2},{3,19},{19,3},{4,20},{20... | collective-permute-start | bytes 8650760 | tf_op jit(solution)/shard_map/ppermute | solution.py:37
  11.5 8.7 %collective-permute-done.2.refs_5_ = bf16[64,5632]{1,0:T(8,128)(2,1)S(1)} collective-permute-done((bf16[64,5632]{1,0:T(8,128)(2,1)}, bf16[64,5632]{1,0:T(8,128)(2,1)S(1)}, u32[]{:S(2)}, u32[]{:S(2)}) %collective-permute-start.2) | collective-permute-done | bytes 720928 | tf_op jit(solution)/shard_map/ppermute | solution.py:37
  20.2 3.6 %collective-permute-start.4 = (bf16[64,5632]{1,0:T(8,128)(2,1)S(1)}, bf16[64,5632]{1,0:T(8,128)(2,1)S(1)}, u32[]{:S(2)}, u32[]{:S(2)}) collective-permute-start(bf16[64,5632]{1,0:T(8,128)(2,1)S(1)} %collective-permute-done.2.refs_5_), channel_id=1, source_target_pairs={{0,136},{16,152},{1,137},{17,153},{2,138},{18,154},{3,139},{19,155... | collective-permute-start | bytes 2162696 | tf_op jit(solution)/shard_map/ppermute | solution.py:37
  23.7 1.3 %collective-permute-start.5 = (bf16[64,5632]{1,0:T(8,128)(2,1)}, bf16[64,5632]{1,0:T(8,128)(2,1)S(1)}, u32[]{:S(2)}, u32[]{:S(2)}) collective-permute-start(bf16[64,5632]{1,0:T(8,128)(2,1)} %collective-permute-done.3.refs_6_), channel_id=1, source_target_pairs={{0,32},{16,48},{1,33},{17,49},{2,34},{18,50},{3,35},{19,51},{4,36}... | collective-permute-start | bytes 2162696 | tf_op jit(solution)/shard_map/ppermute | solution.py:37
  25.1 1.9 %collective-permute-start.6 = (bf16[64,5632]{1,0:T(8,128)(2,1)}, bf16[64,5632]{1,0:T(8,128)(2,1)S(1)}, u32[]{:S(2)}, u32[]{:S(2)}) collective-permute-start(bf16[64,5632]{1,0:T(8,128)(2,1)} %collective-permute-done.1.refs_4_), channel_id=1, source_target_pairs={{0,96},{16,112},{1,97},{17,113},{2,98},{18,114},{3,99},{19,115},{4... | collective-permute-start | bytes 2162696 | tf_op jit(solution)/shard_map/ppermute | solution.py:37
  28.1 11.9 %collective-permute-done.5.refs_1_ = bf16[64,5632]{1,0:T(8,128)(2,1)S(1)} collective-permute-done((bf16[64,5632]{1,0:T(8,128)(2,1)}, bf16[64,5632]{1,0:T(8,128)(2,1)S(1)}, u32[]{:S(2)}, u32[]{:S(2)}) %collective-permute-start.5) | collective-permute-done | bytes 720928 | tf_op jit(solution)/shard_map/ppermute | solution.py:37
  40.0 2.1 %collective-permute-start.7 = (bf16[64,1920]{1,0:T(8,128)(2,1)S(1)}, bf16[64,1920]{1,0:T(8,128)(2,1)S(1)}, u32[]{:S(2)}, u32[]{:S(2)}) collective-permute-start(bf16[64,1920]{1,0:T(8,128)(2,1)S(1)} %slice.34), channel_id=1, source_target_pairs={{0,136},{16,152},{1,137},{17,153},{2,138},{18,154},{3,139},{19,155... | collective-permute-start | bytes 737288 | tf_op jit(solution)/shard_map/ppermute | solution.py:37
  42.5 1.9 %collective-permute-start.9 = (bf16[64,1792]{1,0:T(8,128)(2,1)S(1)}, bf16[64,1792]{1,0:T(8,128)(2,1)S(1)}, u32[]{:S(2)}, u32[]{:S(2)}) collective-permute-start(bf16[64,1792]{1,0:T(8,128)(2,1)S(1)} %slice.36), channel_id=1, source_target_pairs={{0,96},{16,112},{1,97},{17,113},{2,98},{18,114},{3,99},{19,115},{4... | collective-permute-start | bytes 688136 | tf_op jit(solution)/shard_map/ppermute | solution.py:37
  44.5 1.5 %constant_dynamic-update-slice_fusion.4 = bf16[256,5632]{1,0:T(8,128)(2,1)S(1)} fusion(bf16[128,5632]{1,0:T(8,128)(2,1)} %collective-permute-done.10), kind=kLoop, calls=%fused_computation.9 | loop fusion | bytes 2883584
  45.9 3.4 %collective-permute-start.11 = (bf16[128,5632]{1,0:T(8,128)(2,1)}, bf16[128,5632]{1,0:T(8,128)(2,1)S(1)}, u32[]{:S(2)}, u32[]{:S(2)}) collective-permute-start(bf16[128,5632]{1,0:T(8,128)(2,1)} %collective-permute-done.10), channel_id=1, source_target_pairs={{0,16},{16,0},{1,17},{17,1},{2,18},{18,2},{3,19},{19,3},{4,20},{20... | collective-permute-start | bytes 4325384 | tf_op jit(solution)/shard_map/ppermute | solution.py:37
  50.4 3.3 %first_product.1 = (f32[256,256]{1,0:T(8,128)S(1)}, bf16[256,5632]{1,0:T(8,128)(2,1)S(1)}, bf16[256,5632]{1,0:T(8,128)(2,1)S(1)}) custom-call(s32[1]{0:T(128)} %bitcast.which_ref.refs_0_, bf16[128,11264]{1,0:T(8,128)(2,1)} %refs_1_.1, bf16[128,11264]{1,0:T(8,128)(2,1)} %collective-permute-done.refs_2_, bf16[64,5632]{1,0:T(8,128)(2,1)S(1)} %copy-done.1, ...), custom_call_target="tpu_custom_call" | custom-call | flops 3000000000 | bytes 9000000 | tf_op jit(solution)/shard_map/first_product/pallas_call | solution.py:108
  53.7 1.0 %fusion.7.refs_4_ = f32[64,256]{1,0:T(8,128)S(1)} fusion(bf16[64,5632]{1,0:T(8,128)(2,1)S(1)} %constant_dynamic-update-slice_fusion, bf16[256,5632]{1,0:T(8,128)(2,1)S(1)} %get-tuple-element.22), kind=kOutput, calls=%fused_computation.27 | convolution fusion | flops 184549376 | bytes 3670016 | tf_op jit(solution)/shard_map/dot_general | solution.py:41
  54.7 1.1 %fusion.6.refs_3_ = f32[192,256]{1,0:T(8,128)S(1)} fusion(bf16[192,5632]{1,0:T(8,128)(2,1)S(1)} %pack.1, bf16[256,5632]{1,0:T(8,128)(2,1)S(1)} %get-tuple-element.22), kind=kOutput, calls=%fused_computation.26 | convolution fusion | flops 553648128 | bytes 5242880 | tf_op jit(solution)/shard_map/dot_general | solution.py:41
  55.9 1.1 %fusion.9.refs_6_ = f32[192,256]{1,0:T(8,128)S(1)} fusion(bf16[192,5632]{1,0:T(8,128)(2,1)S(1)} %pack.1, bf16[256,5632]{1,0:T(8,128)(2,1)S(1)} %constant_dynamic-update-slice_fusion.3), kind=kOutput, calls=%fused_computation.29 | convolution fusion | flops 553648128 | bytes 5242880 | tf_op jit(solution)/shard_map/dot_general | solution.py:41
  57.0 1.0 %fusion.10.refs_7_ = f32[64,256]{1,0:T(8,128)S(1)} fusion(bf16[64,5632]{1,0:T(8,128)(2,1)S(1)} %constant_dynamic-update-slice_fusion, bf16[256,5632]{1,0:T(8,128)(2,1)S(1)} %constant_dynamic-update-slice_fusion.3), kind=kOutput, calls=%fused_computation.30 | convolution fusion | flops 184549376 | bytes 3670016 | tf_op jit(solution)/shard_map/dot_general | solution.py:41
  58.9 1.4 %symmetrize.1 = (f32[1024,128]{1,0:T(8,128)S(1)}, f32[1032,128]{1,0:T(8,128)S(1)}, f32[8,128]{1,0:T(8,128)S(1)}) custom-call(s32[1,512]{1,0:T(1,128)S(1)} %select_n.66.refs_0_, s32[1024,1]{1,0:T(8,128)S(1)} %copy.5.refs_1_.partner_ref, f32[256,256]{1,0:T(8,128)S(1)} %get-tuple-element.21.refs_2_, f32[192,256]{1,0:T(8,128)S(1)} %fusion.6.refs_3_, ...), custom_call_target="tpu_custom_call" | custom-call | flops 2000000000 | bytes 6000000 | tf_op jit(solution)/shard_map/symmetrize/pallas_call | solution.py:174
  60.3 2.6 %collective-permute-start.12 = (f32[1032,128]{1,0:T(8,128)S(1)}, f32[1032,128]{1,0:T(8,128)S(1)}, u32[]{:S(2)}, u32[]{:S(2)}) collective-permute-start(f32[1032,128]{1,0:T(8,128)S(1)} %get-tuple-element.27), channel_id=1, source_target_pairs={{0,16},{16,0},{1,17},{17,1},{2,18},{18,2},{3,19},{19,3},{4,20},{20... | collective-permute-start | bytes 1585160 | tf_op jit(solution)/shard_map/ppermute | solution.py:37
  62.9 1.5 %collective-permute-done.12 = f32[1032,128]{1,0:T(8,128)S(1)} collective-permute-done((f32[1032,128]{1,0:T(8,128)S(1)}, f32[1032,128]{1,0:T(8,128)S(1)}, u32[]{:S(2)}, u32[]{:S(2)}) %collective-permute-start.12) | collective-permute-done | bytes 528416 | tf_op jit(solution)/shard_map/ppermute | solution.py:37
  64.8 1.3 %reorder.1 = f32[1024,128]{1,0:T(8,128)S(1)} custom-call(s32[1024,1]{1,0:T(8,128)S(1)} %copy.5.refs_1_.partner_ref, f32[1024,128]{1,0:T(8,128)S(1)} %get-tuple-element.30.t_ref), custom_call_target="tpu_custom_call" | custom-call | flops 2000000000 | bytes 6000000 | tf_op jit(solution)/shard_map/reorder/pallas_call | solution.py:191
  66.1 6.3 %collective-permute-done.13 = f16[1040,128]{1,0:T(8,128)(2,1)S(1)} collective-permute-done((f16[1040,128]{1,0:T(8,128)(2,1)S(1)}, f16[1040,128]{1,0:T(8,128)(2,1)S(1)}, u32[]{:S(2)}, u32[]{:S(2)}) %collective-permute-start.13) | collective-permute-done | bytes 266272 | tf_op jit(solution)/shard_map/ppermute | solution.py:37
  (44 shorter events, 4.9 us)
Async XLA Ops:
  0.0 27.0 %copy-start = (s32[16]{0:T(128)S(1)}, s32[16]{0:T(128)}, u32[]{:S(2)}) copy-start(s32[16]{0:T(128)} %param.6) | copy-start | bytes 196
  0.0 27.9 %copy-start.2 = (s32[1024]{0:T(1024)S(1)}, s32[1024]{0:T(1024)}, u32[]{:S(2)}) copy-start(s32[1024]{0:T(1024)} %param.7) | copy-start | bytes 12292
  3.0 17.1 %collective-permute-start.2 = (bf16[64,5632]{1,0:T(8,128)(2,1)}, bf16[64,5632]{1,0:T(8,128)(2,1)S(1)}, u32[]{:S(2)}, u32[]{:S(2)}) collective-permute-start(bf16[64,5632]{1,0:T(8,128)(2,1)} %get-tuple-element.20.refs_3_), channel_id=1, source_target_pairs={{0,32},{16,48},{1,33},{17,49},{2,34},{18,50},{3,35},{19,51},{4,36}... | collective-permute-start | bytes 2162696 | tf_op jit(solution)/shard_map/ppermute | solution.py:37
  5.2 18.5 %collective-permute-start.3 = (bf16[64,5632]{1,0:T(8,128)(2,1)}, bf16[64,5632]{1,0:T(8,128)(2,1)}, u32[]{:S(2)}, u32[]{:S(2)}) collective-permute-start(bf16[64,5632]{1,0:T(8,128)(2,1)} %get-tuple-element.20.refs_3_), channel_id=1, source_target_pairs={{0,96},{16,112},{1,97},{17,113},{2,98},{18,114},{3,99},{19,115},{4... | collective-permute-start | bytes 2162696 | tf_op jit(solution)/shard_map/ppermute | solution.py:37
  7.1 17.9 %collective-permute-start.1 = (bf16[64,5632]{1,0:T(8,128)(2,1)}, bf16[64,5632]{1,0:T(8,128)(2,1)}, u32[]{:S(2)}, u32[]{:S(2)}) collective-permute-start(bf16[64,5632]{1,0:T(8,128)(2,1)} %get-tuple-element.20.refs_3_), channel_id=1, source_target_pairs={{0,136},{16,152},{1,137},{17,153},{2,138},{18,154},{3,139},{19,155... | collective-permute-start | bytes 2162696 | tf_op jit(solution)/shard_map/ppermute | solution.py:37
  9.6 34.8 %collective-permute-start.10 = (bf16[128,5632]{1,0:T(8,128)(2,1)}, bf16[128,5632]{1,0:T(8,128)(2,1)}, u32[]{:S(2)}, u32[]{:S(2)}) collective-permute-start(bf16[128,5632]{1,0:T(8,128)(2,1)} %get-tuple-element.24), channel_id=1, source_target_pairs={{0,8},{16,24},{1,9},{17,25},{2,10},{18,26},{3,11},{19,27},{4,12},{... | collective-permute-start | bytes 4325384 | tf_op jit(solution)/shard_map/ppermute | solution.py:37
  9.6 40.7 %collective-permute-start = (bf16[128,11264]{1,0:T(8,128)(2,1)}, bf16[128,11264]{1,0:T(8,128)(2,1)}, u32[]{:S(2)}, u32[]{:S(2)}) collective-permute-start(bf16[128,11264]{1,0:T(8,128)(2,1)} %refs_1_.1), channel_id=1, source_target_pairs={{0,16},{16,0},{1,17},{17,1},{2,18},{18,2},{3,19},{19,3},{4,20},{20... | collective-permute-start | bytes 8650760 | tf_op jit(solution)/shard_map/ppermute | solution.py:37
  20.2 22.3 %collective-permute-start.4 = (bf16[64,5632]{1,0:T(8,128)(2,1)S(1)}, bf16[64,5632]{1,0:T(8,128)(2,1)S(1)}, u32[]{:S(2)}, u32[]{:S(2)}) collective-permute-start(bf16[64,5632]{1,0:T(8,128)(2,1)S(1)} %collective-permute-done.2.refs_5_), channel_id=1, source_target_pairs={{0,136},{16,152},{1,137},{17,153},{2,138},{18,154},{3,139},{19,155... | collective-permute-start | bytes 2162696 | tf_op jit(solution)/shard_map/ppermute | solution.py:37
  23.7 16.2 %collective-permute-start.5 = (bf16[64,5632]{1,0:T(8,128)(2,1)}, bf16[64,5632]{1,0:T(8,128)(2,1)S(1)}, u32[]{:S(2)}, u32[]{:S(2)}) collective-permute-start(bf16[64,5632]{1,0:T(8,128)(2,1)} %collective-permute-done.3.refs_6_), channel_id=1, source_target_pairs={{0,32},{16,48},{1,33},{17,49},{2,34},{18,50},{3,35},{19,51},{4,36}... | collective-permute-start | bytes 2162696 | tf_op jit(solution)/shard_map/ppermute | solution.py:37
  25.1 17.1 %collective-permute-start.6 = (bf16[64,5632]{1,0:T(8,128)(2,1)}, bf16[64,5632]{1,0:T(8,128)(2,1)S(1)}, u32[]{:S(2)}, u32[]{:S(2)}) collective-permute-start(bf16[64,5632]{1,0:T(8,128)(2,1)} %collective-permute-done.1.refs_4_), channel_id=1, source_target_pairs={{0,96},{16,112},{1,97},{17,113},{2,98},{18,114},{3,99},{19,115},{4... | collective-permute-start | bytes 2162696 | tf_op jit(solution)/shard_map/ppermute | solution.py:37
  40.0 10.2 %collective-permute-start.7 = (bf16[64,1920]{1,0:T(8,128)(2,1)S(1)}, bf16[64,1920]{1,0:T(8,128)(2,1)S(1)}, u32[]{:S(2)}, u32[]{:S(2)}) collective-permute-start(bf16[64,1920]{1,0:T(8,128)(2,1)S(1)} %slice.34), channel_id=1, source_target_pairs={{0,136},{16,152},{1,137},{17,153},{2,138},{18,154},{3,139},{19,155... | collective-permute-start | bytes 737288 | tf_op jit(solution)/shard_map/ppermute | solution.py:37
  42.1 8.1 %collective-permute-start.8 = (bf16[64,1920]{1,0:T(8,128)(2,1)S(1)}, bf16[64,1920]{1,0:T(8,128)(2,1)S(1)}, u32[]{:S(2)}, u32[]{:S(2)}) collective-permute-start(bf16[64,1920]{1,0:T(8,128)(2,1)S(1)} %slice.35), channel_id=1, source_target_pairs={{0,32},{16,48},{1,33},{17,49},{2,34},{18,50},{3,35},{19,51},{4,36}... | collective-permute-start | bytes 737288 | tf_op jit(solution)/shard_map/ppermute | solution.py:37
  42.5 7.8 %collective-permute-start.9 = (bf16[64,1792]{1,0:T(8,128)(2,1)S(1)}, bf16[64,1792]{1,0:T(8,128)(2,1)S(1)}, u32[]{:S(2)}, u32[]{:S(2)}) collective-permute-start(bf16[64,1792]{1,0:T(8,128)(2,1)S(1)} %slice.36), channel_id=1, source_target_pairs={{0,96},{16,112},{1,97},{17,113},{2,98},{18,114},{3,99},{19,115},{4... | collective-permute-start | bytes 688136 | tf_op jit(solution)/shard_map/ppermute | solution.py:37
  45.9 4.4 %copy-start.1 = (bf16[64,5632]{1,0:T(8,128)(2,1)S(1)}, bf16[64,5632]{1,0:T(8,128)(2,1)}, u32[]{:S(2)}) copy-start(bf16[64,5632]{1,0:T(8,128)(2,1)} %get-tuple-element.20.refs_3_) | copy-start | bytes 2162692
  45.9 9.8 %collective-permute-start.11 = (bf16[128,5632]{1,0:T(8,128)(2,1)}, bf16[128,5632]{1,0:T(8,128)(2,1)S(1)}, u32[]{:S(2)}, u32[]{:S(2)}) collective-permute-start(bf16[128,5632]{1,0:T(8,128)(2,1)} %collective-permute-done.10), channel_id=1, source_target_pairs={{0,16},{16,0},{1,17},{17,1},{2,18},{18,2},{3,19},{19,3},{4,20},{20... | collective-permute-start | bytes 4325384 | tf_op jit(solution)/shard_map/ppermute | solution.py:37
  60.3 4.1 %collective-permute-start.12 = (f32[1032,128]{1,0:T(8,128)S(1)}, f32[1032,128]{1,0:T(8,128)S(1)}, u32[]{:S(2)}, u32[]{:S(2)}) collective-permute-start(f32[1032,128]{1,0:T(8,128)S(1)} %get-tuple-element.27), channel_id=1, source_target_pairs={{0,16},{16,0},{1,17},{17,1},{2,18},{18,2},{3,19},{19,3},{4,20},{20... | collective-permute-start | bytes 1585160 | tf_op jit(solution)/shard_map/ppermute | solution.py:37
  64.7 7.7 %collective-permute-start.13 = (f16[1040,128]{1,0:T(8,128)(2,1)S(1)}, f16[1040,128]{1,0:T(8,128)(2,1)S(1)}, u32[]{:S(2)}, u32[]{:S(2)}) collective-permute-start(f16[1040,128]{1,0:T(8,128)(2,1)S(1)} %pad_maximum_fusion), channel_id=1, source_target_pairs={{0,8},{16,24},{1,9},{17,25},{2,10},{18,26},{3,11},{19,27},{4,12},{... | collective-permute-start | bytes 798728 | tf_op jit(solution)/shard_map/ppermute | solution.py:37

commit v3 on v2

--- a/solution.py
+++ b/solution.py
@@ -62,28 +62,22 @@
     return ref.at[:, pl.ds(pl.multiple_of(which * width, width), width)]
 
 
-def split_kernel(which_ref, a_ref, b_ref, keep_ref, give_ref, sem):
-    width = keep_ref.shape[1]
-    which = which_ref[0]
-    keep = pltpu.make_async_copy(columns(a_ref, which, width), keep_ref, sem.at[0])
-    give = pltpu.make_async_copy(columns(b_ref, 1 - which, width), give_ref, sem.at[1])
-    keep.start()
-    give.start()
-    keep.wait()
-    give.wait()
-
-
-def split(which, a, b):
-    half = a.shape[1] // 2
-    return pl.pallas_call(
-        split_kernel,
-        in_specs=[pl.BlockSpec(memory_space=pltpu.SMEM), ANYWHERE, ANYWHERE],
-        out_specs=[WHOLE, WHOLE],
-        out_shape=[jax.ShapeDtypeStruct((t.shape[0], half), t.dtype) for t in (a, b)],
-        scratch_shapes=[pltpu.SemaphoreType.DMA((2,))],
-        cost_estimate=cost(2),
-        name="split",
-    )(which, a, b)
+def half_kernel(which_ref, source_ref, out_ref, sem):
+    copy = pltpu.make_async_copy(columns(source_ref, which_ref[0], out_ref.shape[1]), out_ref, sem)
+    copy.start()
+    copy.wait()
+
+
+def half_of(which, table):
+    return pl.pallas_call(
+        half_kernel,
+        in_specs=[pl.BlockSpec(memory_space=pltpu.SMEM), ANYWHERE],
+        out_specs=WHOLE,
+        out_shape=jax.ShapeDtypeStruct((table.shape[0], table.shape[1] // 2), table.dtype),
+        scratch_shapes=[pltpu.SemaphoreType.DMA],
+        cost_estimate=cost(2),
+        name="half",
+    )(which, table)
 
 
 def first_kernel(n, which_ref, mine_ref, sibling_ref, *refs):
@@ -221,7 +215,8 @@
     slot = jnp.where(alive, blocks[:, None] * height + lane[None, :], -1).reshape(1, -1)
 
     u = {}
-    u[""], given = split(which, amplitudes, integrals)
+    u[""] = jnp.where(which[0] == 1, amplitudes[:, half:], amplitudes[:, :half])
+    given = half_of(1 - which, tied(integrals, u[""]))
     u["a"] = swap(u[""], "x1")
     u["b"] = swap(u[""], "y0")
     u["c"] = swap(u[""], "y1")
@@ -234,11 +229,11 @@
     which, slot, partner = lax.optimization_barrier((which, slot, partner))
     own_first, b_own, first = first_product(which, integrals, b_sib, rows[:4])
     cuts = [0, half * 15 // 44 // 128 * 128, half * 30 // 44 // 128 * 128, half]
-    cut = [u[n][:, cuts[i]:cuts[i + 1]] for i, n in enumerate(("bc", "ac", "ab"))]
+    cut = [tied(u[n], own_first)[:, cuts[i]:cuts[i + 1]] for i, n in enumerate(("bc", "ac", "ab"))]
     last = jnp.concatenate([swap(t, move) for t, move in zip(cut, ("x1", "y0", "y1"))], axis=1)
     b_mate = tied(b_mate, *cut)
     b_mate_sib = swap(b_mate, "core")
-    second = pack(rows[4:])
+    second = pack([tied(r, *cut) for r in rows[4:]])
     own = [own_first, dot_t(second, b_own), dot_t(last, b_own)]
     b_far = jnp.concatenate([b_mate, b_mate_sib], axis=0)
     mate = [dot_t(t, b_far) for t in (first, second, last)]

time: 73.4 us -> 70.8 us (0.965)
  starting transfers between devices: 25.6 us -> 19.5 us
  local copies, waits for them, and re-layouts: 2.82 us -> 4.62 us
  other arithmetic: 1.16 us -> 2.55 us
  waiting for transfers between devices: 28.5 us -> 29.4 us
    ppermute x14, starting transfers between devices: 25.6 us -> 19.5 us  [swap(): return lax.ppermute(block, AXES, pairs)]
    unnamed x9, local copies, waits for them, and re-layouts: 1.51 us -> 3.32 us
    select_n x0 -> x1, other arithmetic: none -> 1.4 us  [shards(): u[''] = jnp.where(which[0] == 1, amplitudes[:, half:], amplitudes[:, :half])]
    ppermute x14, waiting for transfers between devices: 28.5 us -> 29.4 us  [swap(): return lax.ppermute(block, AXES, pairs)]
  transfers between devices with their start and end apart: 14 -> 14, of which waited for: 4 -> 6; matrix products, arithmetic and copies ran while one was open for 7% -> 9% of each run, Pallas kernels for 8% -> 11%
where the time goes in v3:
time: 70.8 us; the launch traced here: 70.6 us
  waiting for transfers between devices  29.4 us (42%)
  starting transfers between devices  19.5 us (28%)
  Pallas kernels  9.25 us (13%)
  matrix products  5.03 us (7%)
  local copies, waits for them, and re-layouts  4.62 us (7%)
  other arithmetic  2.55 us (4%)
    ppermute x14, waiting for transfers between devices, swap(): return lax.ppermute(block, AXES, pairs)  29.4 us
    ppermute x14, starting transfers between devices, swap(): return lax.ppermute(block, AXES, pairs)  19.5 us
    dot_general x5, matrix products, dot_t(): lax.dot_general(a, b, (((1,), (1,)), ((), ())), preferred_element_type=jn...  5.03 us
    unnamed x9, local copies, waits for them, and re-layouts  3.32 us
    pallas_call x1, Pallas kernels, first_product(): pl.pallas_call(lambda *refs: first_kernel(n, *refs), in_specs=[pl.BlockSp...  3.15 us
    pallas_call x1, Pallas kernels, half_of(): pl.pallas_call(half_kernel, in_specs=[pl.BlockSpec(memory_space=pltpu.SME...  2.49 us
    pallas_call x1, Pallas kernels, symmetrize(): pl.pallas_call(lambda *refs: symmetrize_kernel(len(own), *refs), out_shap...  1.44 us
  transfers between devices with their start and end apart: 14, of which 6 were waited for; matrix products, arithmetic and copies ran while one was open for 9% of the time, Pallas kernels for 11%

profile of v3, /device:TPU:1, one launch (start us, length us, event | category | flops | bytes accessed | tf_op | source)
XLA Modules:
  0.0 70.6 jit_solution(16459483531855421084)
XLA Ops:
  0.0 3.2 %collective-permute-start = (bf16[128,11264]{1,0:T(8,128)(2,1)}, bf16[128,11264]{1,0:T(8,128)(2,1)}, u32[]{:S(2)}, u32[]{:S(2)}) collective-permute-start(bf16[128,11264]{1,0:T(8,128)(2,1)} %source_ref), channel_id=1, source_target_pairs={{0,16},{16,0},{1,17},{17,1},{2,18},{18,2},{3,19},{19,3},{4,20},{20... | collective-permute-start | bytes 8650760 | tf_op jit(solution)/shard_map/ppermute | solution.py:37
  3.2 1.4 %slice_select_fusion.refs_3_ = bf16[64,5632]{1,0:T(8,128)(2,1)S(1)} fusion(bf16[64,11264]{1,0:T(8,128)(2,1)} %param.4, pred[]{:T(512)S(6)} %eq.10), kind=kLoop, calls=%fused_computation.1 | loop fusion | flops 360448 | bytes 2162689 | tf_op jit(solution)/shard_map/jit(_where)/select_n | solution.py:218
  5.5 1.3 %collective-permute-start.2 = (bf16[64,5632]{1,0:T(8,128)(2,1)S(1)}, bf16[64,5632]{1,0:T(8,128)(2,1)}, u32[]{:S(2)}, u32[]{:S(2)}) collective-permute-start(bf16[64,5632]{1,0:T(8,128)(2,1)S(1)} %slice_select_fusion.refs_3_), channel_id=1, source_target_pairs={{0,32},{16,48},{1,33},{17,49},{2,34},{18,50},{3,35},{19,51},{4,36}... | collective-permute-start | bytes 2162696 | tf_op jit(solution)/shard_map/ppermute | solution.py:37
  6.8 1.9 %collective-permute-start.3 = (bf16[64,5632]{1,0:T(8,128)(2,1)S(1)}, bf16[64,5632]{1,0:T(8,128)(2,1)}, u32[]{:S(2)}, u32[]{:S(2)}) collective-permute-start(bf16[64,5632]{1,0:T(8,128)(2,1)S(1)} %slice_select_fusion.refs_3_), channel_id=1, source_target_pairs={{0,96},{16,112},{1,97},{17,113},{2,98},{18,114},{3,99},{19,115},{4... | collective-permute-start | bytes 2162696 | tf_op jit(solution)/shard_map/ppermute | solution.py:37
  8.7 2.5 %half.1 = bf16[128,5632]{1,0:T(8,128)(2,1)} custom-call(s32[1]{0:T(128)S(6)} %sub.32.which_ref, bf16[128,11264]{1,0:T(8,128)(2,1)} %source_ref), custom_call_target="tpu_custom_call" | custom-call | flops 2000000000 | bytes 6000000 | tf_op jit(solution)/shard_map/half/pallas_call | solution.py:72
  12.2 10.8 %collective-permute-done.2.refs_5_ = bf16[64,5632]{1,0:T(8,128)(2,1)} collective-permute-done((bf16[64,5632]{1,0:T(8,128)(2,1)S(1)}, bf16[64,5632]{1,0:T(8,128)(2,1)}, u32[]{:S(2)}, u32[]{:S(2)}) %collective-permute-start.2) | collective-permute-done | bytes 720928 | tf_op jit(solution)/shard_map/ppermute | solution.py:37
  23.0 2.0 %collective-permute-start.4 = (bf16[64,5632]{1,0:T(8,128)(2,1)}, bf16[64,5632]{1,0:T(8,128)(2,1)S(1)}, u32[]{:S(2)}, u32[]{:S(2)}) collective-permute-start(bf16[64,5632]{1,0:T(8,128)(2,1)} %collective-permute-done.2.refs_5_), channel_id=1, source_target_pairs={{0,136},{16,152},{1,137},{17,153},{2,138},{18,154},{3,139},{19,155... | collective-permute-start | bytes 2162696 | tf_op jit(solution)/shard_map/ppermute | solution.py:37
  25.3 1.8 %collective-permute-start.6 = (bf16[64,5632]{1,0:T(8,128)(2,1)}, bf16[64,5632]{1,0:T(8,128)(2,1)S(1)}, u32[]{:S(2)}, u32[]{:S(2)}) collective-permute-start(bf16[64,5632]{1,0:T(8,128)(2,1)} %collective-permute-done.1.refs_4_), channel_id=1, source_target_pairs={{0,96},{16,112},{1,97},{17,113},{2,98},{18,114},{3,99},{19,115},{4... | collective-permute-start | bytes 2162696 | tf_op jit(solution)/shard_map/ppermute | solution.py:37
  27.5 1.8 %copy-done.1 = bf16[128,11264]{1,0:T(8,128)(2,1)S(1)} copy-done((bf16[128,11264]{1,0:T(8,128)(2,1)S(1)}, bf16[128,11264]{1,0:T(8,128)(2,1)}, u32[]{:S(2)}) %copy-start.1) | copy-done | bytes 2883608
  29.3 3.1 %first_product.1 = (f32[256,256]{1,0:T(8,128)S(1)}, bf16[256,5632]{1,0:T(8,128)(2,1)S(1)}, bf16[256,5632]{1,0:T(8,128)(2,1)S(1)}) custom-call(s32[1]{0:T(128)} %bitcast.refs_0_, bf16[128,11264]{1,0:T(8,128)(2,1)S(1)} %copy-done.1, bf16[128,11264]{1,0:T(8,128)(2,1)} %collective-permute-done.refs_2_, bf16[64,5632]{1,0:T(8,128)(2,1)S(1)} %slice_select_fusion.refs_3_, ...), custom_call_target="tpu_custom_call" | custom-call | flops 3000000000 | bytes 9000000 | tf_op jit(solution)/shard_map/first_product/pallas_call | solution.py:102
  32.5 9.2 %collective-permute-done.5.refs_1_ = bf16[64,5632]{1,0:T(8,128)(2,1)S(1)} collective-permute-done((bf16[64,5632]{1,0:T(8,128)(2,1)}, bf16[64,5632]{1,0:T(8,128)(2,1)S(1)}, u32[]{:S(2)}, u32[]{:S(2)}) %collective-permute-start.5) | collective-permute-done | bytes 720928 | tf_op jit(solution)/shard_map/ppermute | solution.py:37
  41.7 1.3 %collective-permute-done.6.refs_2_ = bf16[64,5632]{1,0:T(8,128)(2,1)S(1)} collective-permute-done((bf16[64,5632]{1,0:T(8,128)(2,1)}, bf16[64,5632]{1,0:T(8,128)(2,1)S(1)}, u32[]{:S(2)}, u32[]{:S(2)}) %collective-permute-start.6) | collective-permute-done | bytes 720928 | tf_op jit(solution)/shard_map/ppermute | solution.py:37
  43.0 1.4 %collective-permute-start.7 = (bf16[64,1920]{1,0:T(8,128)(2,1)S(1)}, bf16[64,1920]{1,0:T(8,128)(2,1)S(1)}, u32[]{:S(2)}, u32[]{:S(2)}) collective-permute-start(bf16[64,1920]{1,0:T(8,128)(2,1)S(1)} %slice.32), channel_id=1, source_target_pairs={{0,136},{16,152},{1,137},{17,153},{2,138},{18,154},{3,139},{19,155... | collective-permute-start | bytes 737288 | tf_op jit(solution)/shard_map/ppermute | solution.py:37
  44.5 1.9 %collective-permute-start.9 = (bf16[64,1792]{1,0:T(8,128)(2,1)S(1)}, bf16[64,1792]{1,0:T(8,128)(2,1)S(1)}, u32[]{:S(2)}, u32[]{:S(2)}) collective-permute-start(bf16[64,1792]{1,0:T(8,128)(2,1)S(1)} %slice.34), channel_id=1, source_target_pairs={{0,96},{16,112},{1,97},{17,113},{2,98},{18,114},{3,99},{19,115},{4... | collective-permute-start | bytes 688136 | tf_op jit(solution)/shard_map/ppermute | solution.py:37
  46.4 1.5 %constant_dynamic-update-slice_fusion.4 = bf16[256,5632]{1,0:T(8,128)(2,1)S(1)} fusion(bf16[128,5632]{1,0:T(8,128)(2,1)} %collective-permute-done.10), kind=kLoop, calls=%fused_computation.10 | loop fusion | bytes 2883584
  47.8 3.3 %collective-permute-start.11 = (bf16[128,5632]{1,0:T(8,128)(2,1)}, bf16[128,5632]{1,0:T(8,128)(2,1)S(1)}, u32[]{:S(2)}, u32[]{:S(2)}) collective-permute-start(bf16[128,5632]{1,0:T(8,128)(2,1)} %collective-permute-done.10), channel_id=1, source_target_pairs={{0,16},{16,0},{1,17},{17,1},{2,18},{18,2},{3,19},{19,3},{4,20},{20... | collective-permute-start | bytes 4325384 | tf_op jit(solution)/shard_map/ppermute | solution.py:37
  52.1 1.1 %fusion.6.refs_3_ = f32[192,256]{1,0:T(8,128)S(1)} fusion(bf16[192,5632]{1,0:T(8,128)(2,1)S(1)} %pack.1, bf16[256,5632]{1,0:T(8,128)(2,1)S(1)} %get-tuple-element.32), kind=kOutput, calls=%fused_computation.27 | convolution fusion | flops 553648128 | bytes 5242880 | tf_op jit(solution)/shard_map/dot_general | solution.py:41
  53.3 1.0 %fusion.7.refs_4_ = f32[64,256]{1,0:T(8,128)S(1)} fusion(bf16[64,5632]{1,0:T(8,128)(2,1)S(1)} %constant_dynamic-update-slice_fusion, bf16[256,5632]{1,0:T(8,128)(2,1)S(1)} %get-tuple-element.32), kind=kOutput, calls=%fused_computation.28 | convolution fusion | flops 184549376 | bytes 3670016 | tf_op jit(solution)/shard_map/dot_general | solution.py:41
  54.4 1.1 %fusion.9.refs_6_ = f32[192,256]{1,0:T(8,128)S(1)} fusion(bf16[192,5632]{1,0:T(8,128)(2,1)S(1)} %pack.1, bf16[256,5632]{1,0:T(8,128)(2,1)S(1)} %constant_dynamic-update-slice_fusion.3), kind=kOutput, calls=%fused_computation.30 | convolution fusion | flops 553648128 | bytes 5242880 | tf_op jit(solution)/shard_map/dot_general | solution.py:41
  57.4 1.4 %symmetrize.1 = (f32[1024,128]{1,0:T(8,128)S(1)}, f32[1032,128]{1,0:T(8,128)S(1)}, f32[8,128]{1,0:T(8,128)S(1)}) custom-call(s32[1,512]{1,0:T(1,128)S(1)} %select_n.74.refs_0_, s32[1024,1]{1,0:T(8,128)S(1)} %copy.5.refs_1_.partner_ref, f32[256,256]{1,0:T(8,128)S(1)} %get-tuple-element.25.refs_2_, f32[192,256]{1,0:T(8,128)S(1)} %fusion.6.refs_3_, ...), custom_call_target="tpu_custom_call" | custom-call | flops 2000000000 | bytes 6000000 | tf_op jit(solution)/shard_map/symmetrize/pallas_call | solution.py:168
  58.8 1.5 %collective-permute-start.12 = (f32[1032,128]{1,0:T(8,128)S(1)}, f32[1032,128]{1,0:T(8,128)S(1)}, u32[]{:S(2)}, u32[]{:S(2)}) collective-permute-start(f32[1032,128]{1,0:T(8,128)S(1)} %get-tuple-element.37), channel_id=1, source_target_pairs={{0,16},{16,0},{1,17},{17,1},{2,18},{18,2},{3,19},{19,3},{4,20},{20... | collective-permute-start | bytes 1585160 | tf_op jit(solution)/shard_map/ppermute | solution.py:37
  60.3 1.5 %collective-permute-done.12 = f32[1032,128]{1,0:T(8,128)S(1)} collective-permute-done((f32[1032,128]{1,0:T(8,128)S(1)}, f32[1032,128]{1,0:T(8,128)S(1)}, u32[]{:S(2)}, u32[]{:S(2)}) %collective-permute-start.12) | collective-permute-done | bytes 528416 | tf_op jit(solution)/shard_map/ppermute | solution.py:37
  62.1 1.3 %reorder.1 = f32[1024,128]{1,0:T(8,128)S(1)} custom-call(s32[1024,1]{1,0:T(8,128)S(1)} %copy.5.refs_1_.partner_ref, f32[1024,128]{1,0:T(8,128)S(1)} %get-tuple-element.40.t_ref), custom_call_target="tpu_custom_call" | custom-call | flops 2000000000 | bytes 6000000 | tf_op jit(solution)/shard_map/reorder/pallas_call | solution.py:185
  63.4 6.3 %collective-permute-done.13 = f16[1040,128]{1,0:T(8,128)(2,1)S(1)} collective-permute-done((f16[1040,128]{1,0:T(8,128)(2,1)S(1)}, f16[1040,128]{1,0:T(8,128)(2,1)S(1)}, u32[]{:S(2)}, u32[]{:S(2)}) %collective-permute-start.13) | collective-permute-done | bytes 266272 | tf_op jit(solution)/shard_map/ppermute | solution.py:37
  (45 shorter events, 6.7 us)
Async XLA Ops:
  0.0 11.5 %copy-start = (s32[16]{0:T(128)S(1)}, s32[16]{0:T(128)}, u32[]{:S(2)}) copy-start(s32[16]{0:T(128)} %param.6) | copy-start | bytes 196
  0.0 27.5 %collective-permute-start = (bf16[128,11264]{1,0:T(8,128)(2,1)}, bf16[128,11264]{1,0:T(8,128)(2,1)}, u32[]{:S(2)}, u32[]{:S(2)}) collective-permute-start(bf16[128,11264]{1,0:T(8,128)(2,1)} %source_ref), channel_id=1, source_target_pairs={{0,16},{16,0},{1,17},{17,1},{2,18},{18,2},{3,19},{19,3},{4,20},{20... | collective-permute-start | bytes 8650760 | tf_op jit(solution)/shard_map/ppermute | solution.py:37
  4.7 20.6 %collective-permute-start.1 = (bf16[64,5632]{1,0:T(8,128)(2,1)S(1)}, bf16[64,5632]{1,0:T(8,128)(2,1)}, u32[]{:S(2)}, u32[]{:S(2)}) collective-permute-start(bf16[64,5632]{1,0:T(8,128)(2,1)S(1)} %slice_select_fusion.refs_3_), channel_id=1, source_target_pairs={{0,136},{16,152},{1,137},{17,153},{2,138},{18,154},{3,139},{19,155... | collective-permute-start | bytes 2162696 | tf_op jit(solution)/shard_map/ppermute | solution.py:37
  5.5 17.5 %collective-permute-start.2 = (bf16[64,5632]{1,0:T(8,128)(2,1)S(1)}, bf16[64,5632]{1,0:T(8,128)(2,1)}, u32[]{:S(2)}, u32[]{:S(2)}) collective-permute-start(bf16[64,5632]{1,0:T(8,128)(2,1)S(1)} %slice_select_fusion.refs_3_), channel_id=1, source_target_pairs={{0,32},{16,48},{1,33},{17,49},{2,34},{18,50},{3,35},{19,51},{4,36}... | collective-permute-start | bytes 2162696 | tf_op jit(solution)/shard_map/ppermute | solution.py:37
  6.8 18.4 %collective-permute-start.3 = (bf16[64,5632]{1,0:T(8,128)(2,1)S(1)}, bf16[64,5632]{1,0:T(8,128)(2,1)}, u32[]{:S(2)}, u32[]{:S(2)}) collective-permute-start(bf16[64,5632]{1,0:T(8,128)(2,1)S(1)} %slice_select_fusion.refs_3_), channel_id=1, source_target_pairs={{0,96},{16,112},{1,97},{17,113},{2,98},{18,114},{3,99},{19,115},{4... | collective-permute-start | bytes 2162696 | tf_op jit(solution)/shard_map/ppermute | solution.py:37
  8.7 18.6 %copy-start.2 = (s32[1024]{0:T(1024)S(1)}, s32[1024]{0:T(1024)}, u32[]{:S(2)}) copy-start(s32[1024]{0:T(1024)} %param.7) | copy-start | bytes 12292
  11.2 35.2 %collective-permute-start.10 = (bf16[128,5632]{1,0:T(8,128)(2,1)}, bf16[128,5632]{1,0:T(8,128)(2,1)}, u32[]{:S(2)}, u32[]{:S(2)}) collective-permute-start(bf16[128,5632]{1,0:T(8,128)(2,1)} %half.1), channel_id=1, source_target_pairs={{0,8},{16,24},{1,9},{17,25},{2,10},{18,26},{3,11},{19,27},{4,12},{... | collective-permute-start | bytes 4325384 | tf_op jit(solution)/shard_map/ppermute | solution.py:37
  23.0 20.0 %collective-permute-start.4 = (bf16[64,5632]{1,0:T(8,128)(2,1)}, bf16[64,5632]{1,0:T(8,128)(2,1)S(1)}, u32[]{:S(2)}, u32[]{:S(2)}) collective-permute-start(bf16[64,5632]{1,0:T(8,128)(2,1)} %collective-permute-done.2.refs_5_), channel_id=1, source_target_pairs={{0,136},{16,152},{1,137},{17,153},{2,138},{18,154},{3,139},{19,155... | collective-permute-start | bytes 2162696 | tf_op jit(solution)/shard_map/ppermute | solution.py:37
  25.2 16.5 %collective-permute-start.5 = (bf16[64,5632]{1,0:T(8,128)(2,1)}, bf16[64,5632]{1,0:T(8,128)(2,1)S(1)}, u32[]{:S(2)}, u32[]{:S(2)}) collective-permute-start(bf16[64,5632]{1,0:T(8,128)(2,1)} %collective-permute-done.3.refs_6_), channel_id=1, source_target_pairs={{0,32},{16,48},{1,33},{17,49},{2,34},{18,50},{3,35},{19,51},{4,36}... | collective-permute-start | bytes 2162696 | tf_op jit(solution)/shard_map/ppermute | solution.py:37
  25.3 17.7 %collective-permute-start.6 = (bf16[64,5632]{1,0:T(8,128)(2,1)}, bf16[64,5632]{1,0:T(8,128)(2,1)S(1)}, u32[]{:S(2)}, u32[]{:S(2)}) collective-permute-start(bf16[64,5632]{1,0:T(8,128)(2,1)} %collective-permute-done.1.refs_4_), channel_id=1, source_target_pairs={{0,96},{16,112},{1,97},{17,113},{2,98},{18,114},{3,99},{19,115},{4... | collective-permute-start | bytes 2162696 | tf_op jit(solution)/shard_map/ppermute | solution.py:37
  27.5 1.8 %copy-start.1 = (bf16[128,11264]{1,0:T(8,128)(2,1)S(1)}, bf16[128,11264]{1,0:T(8,128)(2,1)}, u32[]{:S(2)}) copy-start(bf16[128,11264]{1,0:T(8,128)(2,1)} %source_ref) | copy-start | bytes 8650756
  43.0 10.1 %collective-permute-start.7 = (bf16[64,1920]{1,0:T(8,128)(2,1)S(1)}, bf16[64,1920]{1,0:T(8,128)(2,1)S(1)}, u32[]{:S(2)}, u32[]{:S(2)}) collective-permute-start(bf16[64,1920]{1,0:T(8,128)(2,1)S(1)} %slice.32), channel_id=1, source_target_pairs={{0,136},{16,152},{1,137},{17,153},{2,138},{18,154},{3,139},{19,155... | collective-permute-start | bytes 737288 | tf_op jit(solution)/shard_map/ppermute | solution.py:37
  44.5 8.7 %collective-permute-start.8 = (bf16[64,1920]{1,0:T(8,128)(2,1)S(1)}, bf16[64,1920]{1,0:T(8,128)(2,1)S(1)}, u32[]{:S(2)}, u32[]{:S(2)}) collective-permute-start(bf16[64,1920]{1,0:T(8,128)(2,1)S(1)} %slice.33), channel_id=1, source_target_pairs={{0,32},{16,48},{1,33},{17,49},{2,34},{18,50},{3,35},{19,51},{4,36}... | collective-permute-start | bytes 737288 | tf_op jit(solution)/shard_map/ppermute | solution.py:37
  44.5 8.8 %collective-permute-start.9 = (bf16[64,1792]{1,0:T(8,128)(2,1)S(1)}, bf16[64,1792]{1,0:T(8,128)(2,1)S(1)}, u32[]{:S(2)}, u32[]{:S(2)}) collective-permute-start(bf16[64,1792]{1,0:T(8,128)(2,1)S(1)} %slice.34), channel_id=1, source_target_pairs={{0,96},{16,112},{1,97},{17,113},{2,98},{18,114},{3,99},{19,115},{4... | collective-permute-start | bytes 688136 | tf_op jit(solution)/shard_map/ppermute | solution.py:37
  47.8 6.4 %collective-permute-start.11 = (bf16[128,5632]{1,0:T(8,128)(2,1)}, bf16[128,5632]{1,0:T(8,128)(2,1)S(1)}, u32[]{:S(2)}, u32[]{:S(2)}) collective-permute-start(bf16[128,5632]{1,0:T(8,128)(2,1)} %collective-permute-done.10), channel_id=1, source_target_pairs={{0,16},{16,0},{1,17},{17,1},{2,18},{18,2},{3,19},{19,3},{4,20},{20... | collective-permute-start | bytes 4325384 | tf_op jit(solution)/shard_map/ppermute | solution.py:37
  58.8 3.0 %collective-permute-start.12 = (f32[1032,128]{1,0:T(8,128)S(1)}, f32[1032,128]{1,0:T(8,128)S(1)}, u32[]{:S(2)}, u32[]{:S(2)}) collective-permute-start(f32[1032,128]{1,0:T(8,128)S(1)} %get-tuple-element.37), channel_id=1, source_target_pairs={{0,16},{16,0},{1,17},{17,1},{2,18},{18,2},{3,19},{19,3},{4,20},{20... | collective-permute-start | bytes 1585160 | tf_op jit(solution)/shard_map/ppermute | solution.py:37
  62.0 7.7 %collective-permute-start.13 = (f16[1040,128]{1,0:T(8,128)(2,1)S(1)}, f16[1040,128]{1,0:T(8,128)(2,1)S(1)}, u32[]{:S(2)}, u32[]{:S(2)}) collective-permute-start(f16[1040,128]{1,0:T(8,128)(2,1)S(1)} %pad_maximum_fusion), channel_id=1, source_target_pairs={{0,8},{16,24},{1,9},{17,25},{2,10},{18,26},{3,11},{19,27},{4,12},{... | collective-permute-start | bytes 798728 | tf_op jit(solution)/shard_map/ppermute | solution.py:37

commit v4 on v3

--- a/solution.py
+++ b/solution.py
@@ -228,7 +228,7 @@
     rows = [u[n] for n in names[:7]]
     which, slot, partner = lax.optimization_barrier((which, slot, partner))
     own_first, b_own, first = first_product(which, integrals, b_sib, rows[:4])
-    cuts = [0, half * 15 // 44 // 128 * 128, half * 30 // 44 // 128 * 128, half]
+    cuts = [0, half * 16 // 44 // 128 * 128, half * 32 // 44 // 128 * 128, half]
     cut = [tied(u[n], own_first)[:, cuts[i]:cuts[i + 1]] for i, n in enumerate(("bc", "ac", "ab"))]
     last = jnp.concatenate([swap(t, move) for t, move in zip(cut, ("x1", "y0", "y1"))], axis=1)
     b_mate = tied(b_mate, *cut)

time: 70.8 us -> 70.5 us (level)
  no operation moved by 1% of the time
where the time goes in v4:
time: 70.5 us; the launch traced here: 70.2 us
  waiting for transfers between devices  29.4 us (42%)
  starting transfers between devices  19.1 us (27%)
  Pallas kernels  9.25 us (13%)
  matrix products  5.03 us (7%)
  local copies, waits for them, and re-layouts  4.61 us (7%)
  other arithmetic  2.55 us (4%)
    ppermute x14, waiting for transfers between devices, swap(): return lax.ppermute(block, AXES, pairs)  29.4 us
    ppermute x14, starting transfers between devices, swap(): return lax.ppermute(block, AXES, pairs)  19.1 us
    dot_general x5, matrix products, dot_t(): lax.dot_general(a, b, (((1,), (1,)), ((), ())), preferred_element_type=jn...  5.03 us
    unnamed x9, local copies, waits for them, and re-layouts  3.31 us
    pallas_call x1, Pallas kernels, first_product(): pl.pallas_call(lambda *refs: first_kernel(n, *refs), in_specs=[pl.BlockSp...  3.15 us
    pallas_call x1, Pallas kernels, half_of(): pl.pallas_call(half_kernel, in_specs=[pl.BlockSpec(memory_space=pltpu.SME...  2.49 us
    pallas_call x1, Pallas kernels, symmetrize(): pl.pallas_call(lambda *refs: symmetrize_kernel(len(own), *refs), out_shap...  1.44 us
  transfers between devices with their start and end apart: 14, of which 6 were waited for; matrix products, arithmetic and copies ran while one was open for 9% of the time, Pallas kernels for 11%

profile of v4, /device:TPU:1, one launch (start us, length us, event | category | flops | bytes accessed | tf_op | source)
XLA Modules:
  0.0 70.2 jit_solution(1408712217910395204)
XLA Ops:
  0.0 3.2 %collective-permute-start = (bf16[128,11264]{1,0:T(8,128)(2,1)}, bf16[128,11264]{1,0:T(8,128)(2,1)}, u32[]{:S(2)}, u32[]{:S(2)}) collective-permute-start(bf16[128,11264]{1,0:T(8,128)(2,1)} %source_ref), channel_id=1, source_target_pairs={{0,16},{16,0},{1,17},{17,1},{2,18},{18,2},{3,19},{19,3},{4,20},{20... | collective-permute-start | bytes 8650760 | tf_op jit(solution)/shard_map/ppermute | solution.py:37
  3.2 1.4 %slice_select_fusion.refs_3_ = bf16[64,5632]{1,0:T(8,128)(2,1)S(1)} fusion(bf16[64,11264]{1,0:T(8,128)(2,1)} %param.4, pred[]{:T(512)S(6)} %eq.10), kind=kLoop, calls=%fused_computation.1 | loop fusion | flops 360448 | bytes 2162689 | tf_op jit(solution)/shard_map/jit(_where)/select_n | solution.py:218
  5.5 1.3 %collective-permute-start.2 = (bf16[64,5632]{1,0:T(8,128)(2,1)S(1)}, bf16[64,5632]{1,0:T(8,128)(2,1)}, u32[]{:S(2)}, u32[]{:S(2)}) collective-permute-start(bf16[64,5632]{1,0:T(8,128)(2,1)S(1)} %slice_select_fusion.refs_3_), channel_id=1, source_target_pairs={{0,32},{16,48},{1,33},{17,49},{2,34},{18,50},{3,35},{19,51},{4,36}... | collective-permute-start | bytes 2162696 | tf_op jit(solution)/shard_map/ppermute | solution.py:37
  6.8 1.9 %collective-permute-start.3 = (bf16[64,5632]{1,0:T(8,128)(2,1)S(1)}, bf16[64,5632]{1,0:T(8,128)(2,1)}, u32[]{:S(2)}, u32[]{:S(2)}) collective-permute-start(bf16[64,5632]{1,0:T(8,128)(2,1)S(1)} %slice_select_fusion.refs_3_), channel_id=1, source_target_pairs={{0,96},{16,112},{1,97},{17,113},{2,98},{18,114},{3,99},{19,115},{4... | collective-permute-start | bytes 2162696 | tf_op jit(solution)/shard_map/ppermute | solution.py:37
  8.7 2.5 %half.1 = bf16[128,5632]{1,0:T(8,128)(2,1)} custom-call(s32[1]{0:T(128)S(6)} %sub.32.which_ref, bf16[128,11264]{1,0:T(8,128)(2,1)} %source_ref), custom_call_target="tpu_custom_call" | custom-call | flops 2000000000 | bytes 6000000 | tf_op jit(solution)/shard_map/half/pallas_call | solution.py:72
  12.2 10.8 %collective-permute-done.2.refs_5_ = bf16[64,5632]{1,0:T(8,128)(2,1)} collective-permute-done((bf16[64,5632]{1,0:T(8,128)(2,1)S(1)}, bf16[64,5632]{1,0:T(8,128)(2,1)}, u32[]{:S(2)}, u32[]{:S(2)}) %collective-permute-start.2) | collective-permute-done | bytes 720928 | tf_op jit(solution)/shard_map/ppermute | solution.py:37
  23.0 2.0 %collective-permute-start.4 = (bf16[64,5632]{1,0:T(8,128)(2,1)}, bf16[64,5632]{1,0:T(8,128)(2,1)S(1)}, u32[]{:S(2)}, u32[]{:S(2)}) collective-permute-start(bf16[64,5632]{1,0:T(8,128)(2,1)} %collective-permute-done.2.refs_5_), channel_id=1, source_target_pairs={{0,136},{16,152},{1,137},{17,153},{2,138},{18,154},{3,139},{19,155... | collective-permute-start | bytes 2162696 | tf_op jit(solution)/shard_map/ppermute | solution.py:37
  25.3 1.8 %collective-permute-start.6 = (bf16[64,5632]{1,0:T(8,128)(2,1)}, bf16[64,5632]{1,0:T(8,128)(2,1)S(1)}, u32[]{:S(2)}, u32[]{:S(2)}) collective-permute-start(bf16[64,5632]{1,0:T(8,128)(2,1)} %collective-permute-done.1.refs_4_), channel_id=1, source_target_pairs={{0,96},{16,112},{1,97},{17,113},{2,98},{18,114},{3,99},{19,115},{4... | collective-permute-start | bytes 2162696 | tf_op jit(solution)/shard_map/ppermute | solution.py:37
  27.5 1.8 %copy-done.1 = bf16[128,11264]{1,0:T(8,128)(2,1)S(1)} copy-done((bf16[128,11264]{1,0:T(8,128)(2,1)S(1)}, bf16[128,11264]{1,0:T(8,128)(2,1)}, u32[]{:S(2)}) %copy-start.1) | copy-done | bytes 2883608
  29.3 3.1 %first_product.1 = (f32[256,256]{1,0:T(8,128)S(1)}, bf16[256,5632]{1,0:T(8,128)(2,1)S(1)}, bf16[256,5632]{1,0:T(8,128)(2,1)S(1)}) custom-call(s32[1]{0:T(128)} %bitcast.refs_0_, bf16[128,11264]{1,0:T(8,128)(2,1)S(1)} %copy-done.1, bf16[128,11264]{1,0:T(8,128)(2,1)} %collective-permute-done.refs_2_, bf16[64,5632]{1,0:T(8,128)(2,1)S(1)} %slice_select_fusion.refs_3_, ...), custom_call_target="tpu_custom_call" | custom-call | flops 3000000000 | bytes 9000000 | tf_op jit(solution)/shard_map/first_product/pallas_call | solution.py:102
  32.5 9.2 %collective-permute-done.5.refs_1_ = bf16[64,5632]{1,0:T(8,128)(2,1)S(1)} collective-permute-done((bf16[64,5632]{1,0:T(8,128)(2,1)}, bf16[64,5632]{1,0:T(8,128)(2,1)S(1)}, u32[]{:S(2)}, u32[]{:S(2)}) %collective-permute-start.5) | collective-permute-done | bytes 720928 | tf_op jit(solution)/shard_map/ppermute | solution.py:37
  41.7 1.3 %collective-permute-done.6.refs_2_ = bf16[64,5632]{1,0:T(8,128)(2,1)S(1)} collective-permute-done((bf16[64,5632]{1,0:T(8,128)(2,1)}, bf16[64,5632]{1,0:T(8,128)(2,1)S(1)}, u32[]{:S(2)}, u32[]{:S(2)}) %collective-permute-start.6) | collective-permute-done | bytes 720928 | tf_op jit(solution)/shard_map/ppermute | solution.py:37
  43.0 1.4 %collective-permute-start.7 = (bf16[64,2048]{1,0:T(8,128)(2,1)S(1)}, bf16[64,2048]{1,0:T(8,128)(2,1)S(1)}, u32[]{:S(2)}, u32[]{:S(2)}) collective-permute-start(bf16[64,2048]{1,0:T(8,128)(2,1)S(1)} %slice.32), channel_id=1, source_target_pairs={{0,136},{16,152},{1,137},{17,153},{2,138},{18,154},{3,139},{19,155... | collective-permute-start | bytes 786440 | tf_op jit(solution)/shard_map/ppermute | solution.py:37
  44.5 1.9 %collective-permute-start.9 = (bf16[64,1536]{1,0:T(8,128)(2,1)S(1)}, bf16[64,1536]{1,0:T(8,128)(2,1)S(1)}, u32[]{:S(2)}, u32[]{:S(2)}) collective-permute-start(bf16[64,1536]{1,0:T(8,128)(2,1)S(1)} %slice.34), channel_id=1, source_target_pairs={{0,96},{16,112},{1,97},{17,113},{2,98},{18,114},{3,99},{19,115},{4... | collective-permute-start | bytes 589832 | tf_op jit(solution)/shard_map/ppermute | solution.py:37
  46.4 1.5 %constant_dynamic-update-slice_fusion.4 = bf16[256,5632]{1,0:T(8,128)(2,1)S(1)} fusion(bf16[128,5632]{1,0:T(8,128)(2,1)} %collective-permute-done.10), kind=kLoop, calls=%fused_computation.10 | loop fusion | bytes 2883584
  47.8 3.3 %collective-permute-start.11 = (bf16[128,5632]{1,0:T(8,128)(2,1)}, bf16[128,5632]{1,0:T(8,128)(2,1)S(1)}, u32[]{:S(2)}, u32[]{:S(2)}) collective-permute-start(bf16[128,5632]{1,0:T(8,128)(2,1)} %collective-permute-done.10), channel_id=1, source_target_pairs={{0,16},{16,0},{1,17},{17,1},{2,18},{18,2},{3,19},{19,3},{4,20},{20... | collective-permute-start | bytes 4325384 | tf_op jit(solution)/shard_map/ppermute | solution.py:37
  52.1 1.1 %fusion.6.refs_3_ = f32[192,256]{1,0:T(8,128)S(1)} fusion(bf16[192,5632]{1,0:T(8,128)(2,1)S(1)} %pack.1, bf16[256,5632]{1,0:T(8,128)(2,1)S(1)} %get-tuple-element.32), kind=kOutput, calls=%fused_computation.27 | convolution fusion | flops 553648128 | bytes 5242880 | tf_op jit(solution)/shard_map/dot_general | solution.py:41
  53.3 1.0 %fusion.7.refs_4_ = f32[64,256]{1,0:T(8,128)S(1)} fusion(bf16[64,5632]{1,0:T(8,128)(2,1)S(1)} %constant_dynamic-update-slice_fusion, bf16[256,5632]{1,0:T(8,128)(2,1)S(1)} %get-tuple-element.32), kind=kOutput, calls=%fused_computation.28 | convolution fusion | flops 184549376 | bytes 3670016 | tf_op jit(solution)/shard_map/dot_general | solution.py:41
  54.4 1.1 %fusion.9.refs_6_ = f32[192,256]{1,0:T(8,128)S(1)} fusion(bf16[192,5632]{1,0:T(8,128)(2,1)S(1)} %pack.1, bf16[256,5632]{1,0:T(8,128)(2,1)S(1)} %constant_dynamic-update-slice_fusion.3), kind=kOutput, calls=%fused_computation.30 | convolution fusion | flops 553648128 | bytes 5242880 | tf_op jit(solution)/shard_map/dot_general | solution.py:41
  57.4 1.4 %symmetrize.1 = (f32[1024,128]{1,0:T(8,128)S(1)}, f32[1032,128]{1,0:T(8,128)S(1)}, f32[8,128]{1,0:T(8,128)S(1)}) custom-call(s32[1,512]{1,0:T(1,128)S(1)} %select_n.74.refs_0_, s32[1024,1]{1,0:T(8,128)S(1)} %copy.5.refs_1_.partner_ref, f32[256,256]{1,0:T(8,128)S(1)} %get-tuple-element.25.refs_2_, f32[192,256]{1,0:T(8,128)S(1)} %fusion.6.refs_3_, ...), custom_call_target="tpu_custom_call" | custom-call | flops 2000000000 | bytes 6000000 | tf_op jit(solution)/shard_map/symmetrize/pallas_call | solution.py:168
  58.8 1.1 %collective-permute-start.12 = (f32[1032,128]{1,0:T(8,128)S(1)}, f32[1032,128]{1,0:T(8,128)S(1)}, u32[]{:S(2)}, u32[]{:S(2)}) collective-permute-start(f32[1032,128]{1,0:T(8,128)S(1)} %get-tuple-element.37), channel_id=1, source_target_pairs={{0,16},{16,0},{1,17},{17,1},{2,18},{18,2},{3,19},{19,3},{4,20},{20... | collective-permute-start | bytes 1585160 | tf_op jit(solution)/shard_map/ppermute | solution.py:37
  59.9 1.5 %collective-permute-done.12 = f32[1032,128]{1,0:T(8,128)S(1)} collective-permute-done((f32[1032,128]{1,0:T(8,128)S(1)}, f32[1032,128]{1,0:T(8,128)S(1)}, u32[]{:S(2)}, u32[]{:S(2)}) %collective-permute-start.12) | collective-permute-done | bytes 528416 | tf_op jit(solution)/shard_map/ppermute | solution.py:37
  61.8 1.3 %reorder.1 = f32[1024,128]{1,0:T(8,128)S(1)} custom-call(s32[1024,1]{1,0:T(8,128)S(1)} %copy.5.refs_1_.partner_ref, f32[1024,128]{1,0:T(8,128)S(1)} %get-tuple-element.40.t_ref), custom_call_target="tpu_custom_call" | custom-call | flops 2000000000 | bytes 6000000 | tf_op jit(solution)/shard_map/reorder/pallas_call | solution.py:185
  63.1 6.3 %collective-permute-done.13 = f16[1040,128]{1,0:T(8,128)(2,1)S(1)} collective-permute-done((f16[1040,128]{1,0:T(8,128)(2,1)S(1)}, f16[1040,128]{1,0:T(8,128)(2,1)S(1)}, u32[]{:S(2)}, u32[]{:S(2)}) %collective-permute-start.13) | collective-permute-done | bytes 266272 | tf_op jit(solution)/shard_map/ppermute | solution.py:37
  (45 shorter events, 6.7 us)
Async XLA Ops:
  0.0 11.5 %copy-start = (s32[16]{0:T(128)S(1)}, s32[16]{0:T(128)}, u32[]{:S(2)}) copy-start(s32[16]{0:T(128)} %param.6) | copy-start | bytes 196
  0.0 27.5 %collective-permute-start = (bf16[128,11264]{1,0:T(8,128)(2,1)}, bf16[128,11264]{1,0:T(8,128)(2,1)}, u32[]{:S(2)}, u32[]{:S(2)}) collective-permute-start(bf16[128,11264]{1,0:T(8,128)(2,1)} %source_ref), channel_id=1, source_target_pairs={{0,16},{16,0},{1,17},{17,1},{2,18},{18,2},{3,19},{19,3},{4,20},{20... | collective-permute-start | bytes 8650760 | tf_op jit(solution)/shard_map/ppermute | solution.py:37
  4.7 20.6 %collective-permute-start.1 = (bf16[64,5632]{1,0:T(8,128)(2,1)S(1)}, bf16[64,5632]{1,0:T(8,128)(2,1)}, u32[]{:S(2)}, u32[]{:S(2)}) collective-permute-start(bf16[64,5632]{1,0:T(8,128)(2,1)S(1)} %slice_select_fusion.refs_3_), channel_id=1, source_target_pairs={{0,136},{16,152},{1,137},{17,153},{2,138},{18,154},{3,139},{19,155... | collective-permute-start | bytes 2162696 | tf_op jit(solution)/shard_map/ppermute | solution.py:37
  5.5 17.5 %collective-permute-start.2 = (bf16[64,5632]{1,0:T(8,128)(2,1)S(1)}, bf16[64,5632]{1,0:T(8,128)(2,1)}, u32[]{:S(2)}, u32[]{:S(2)}) collective-permute-start(bf16[64,5632]{1,0:T(8,128)(2,1)S(1)} %slice_select_fusion.refs_3_), channel_id=1, source_target_pairs={{0,32},{16,48},{1,33},{17,49},{2,34},{18,50},{3,35},{19,51},{4,36}... | collective-permute-start | bytes 2162696 | tf_op jit(solution)/shard_map/ppermute | solution.py:37
  6.8 18.4 %collective-permute-start.3 = (bf16[64,5632]{1,0:T(8,128)(2,1)S(1)}, bf16[64,5632]{1,0:T(8,128)(2,1)}, u32[]{:S(2)}, u32[]{:S(2)}) collective-permute-start(bf16[64,5632]{1,0:T(8,128)(2,1)S(1)} %slice_select_fusion.refs_3_), channel_id=1, source_target_pairs={{0,96},{16,112},{1,97},{17,113},{2,98},{18,114},{3,99},{19,115},{4... | collective-permute-start | bytes 2162696 | tf_op jit(solution)/shard_map/ppermute | solution.py:37
  8.7 18.6 %copy-start.2 = (s32[1024]{0:T(1024)S(1)}, s32[1024]{0:T(1024)}, u32[]{:S(2)}) copy-start(s32[1024]{0:T(1024)} %param.7) | copy-start | bytes 12292
  11.2 35.2 %collective-permute-start.10 = (bf16[128,5632]{1,0:T(8,128)(2,1)}, bf16[128,5632]{1,0:T(8,128)(2,1)}, u32[]{:S(2)}, u32[]{:S(2)}) collective-permute-start(bf16[128,5632]{1,0:T(8,128)(2,1)} %half.1), channel_id=1, source_target_pairs={{0,8},{16,24},{1,9},{17,25},{2,10},{18,26},{3,11},{19,27},{4,12},{... | collective-permute-start | bytes 4325384 | tf_op jit(solution)/shard_map/ppermute | solution.py:37
  23.0 20.0 %collective-permute-start.4 = (bf16[64,5632]{1,0:T(8,128)(2,1)}, bf16[64,5632]{1,0:T(8,128)(2,1)S(1)}, u32[]{:S(2)}, u32[]{:S(2)}) collective-permute-start(bf16[64,5632]{1,0:T(8,128)(2,1)} %collective-permute-done.2.refs_5_), channel_id=1, source_target_pairs={{0,136},{16,152},{1,137},{17,153},{2,138},{18,154},{3,139},{19,155... | collective-permute-start | bytes 2162696 | tf_op jit(solution)/shard_map/ppermute | solution.py:37
  25.2 16.5 %collective-permute-start.5 = (bf16[64,5632]{1,0:T(8,128)(2,1)}, bf16[64,5632]{1,0:T(8,128)(2,1)S(1)}, u32[]{:S(2)}, u32[]{:S(2)}) collective-permute-start(bf16[64,5632]{1,0:T(8,128)(2,1)} %collective-permute-done.3.refs_6_), channel_id=1, source_target_pairs={{0,32},{16,48},{1,33},{17,49},{2,34},{18,50},{3,35},{19,51},{4,36}... | collective-permute-start | bytes 2162696 | tf_op jit(solution)/shard_map/ppermute | solution.py:37
  25.3 17.7 %collective-permute-start.6 = (bf16[64,5632]{1,0:T(8,128)(2,1)}, bf16[64,5632]{1,0:T(8,128)(2,1)S(1)}, u32[]{:S(2)}, u32[]{:S(2)}) collective-permute-start(bf16[64,5632]{1,0:T(8,128)(2,1)} %collective-permute-done.1.refs_4_), channel_id=1, source_target_pairs={{0,96},{16,112},{1,97},{17,113},{2,98},{18,114},{3,99},{19,115},{4... | collective-permute-start | bytes 2162696 | tf_op jit(solution)/shard_map/ppermute | solution.py:37
  27.5 1.8 %copy-start.1 = (bf16[128,11264]{1,0:T(8,128)(2,1)S(1)}, bf16[128,11264]{1,0:T(8,128)(2,1)}, u32[]{:S(2)}) copy-start(bf16[128,11264]{1,0:T(8,128)(2,1)} %source_ref) | copy-start | bytes 8650756
  43.0 10.1 %collective-permute-start.7 = (bf16[64,2048]{1,0:T(8,128)(2,1)S(1)}, bf16[64,2048]{1,0:T(8,128)(2,1)S(1)}, u32[]{:S(2)}, u32[]{:S(2)}) collective-permute-start(bf16[64,2048]{1,0:T(8,128)(2,1)S(1)} %slice.32), channel_id=1, source_target_pairs={{0,136},{16,152},{1,137},{17,153},{2,138},{18,154},{3,139},{19,155... | collective-permute-start | bytes 786440 | tf_op jit(solution)/shard_map/ppermute | solution.py:37
  44.5 8.7 %collective-permute-start.8 = (bf16[64,2048]{1,0:T(8,128)(2,1)S(1)}, bf16[64,2048]{1,0:T(8,128)(2,1)S(1)}, u32[]{:S(2)}, u32[]{:S(2)}) collective-permute-start(bf16[64,2048]{1,0:T(8,128)(2,1)S(1)} %slice.33), channel_id=1, source_target_pairs={{0,32},{16,48},{1,33},{17,49},{2,34},{18,50},{3,35},{19,51},{4,36}... | collective-permute-start | bytes 786440 | tf_op jit(solution)/shard_map/ppermute | solution.py:37
  44.5 8.7 %collective-permute-start.9 = (bf16[64,1536]{1,0:T(8,128)(2,1)S(1)}, bf16[64,1536]{1,0:T(8,128)(2,1)S(1)}, u32[]{:S(2)}, u32[]{:S(2)}) collective-permute-start(bf16[64,1536]{1,0:T(8,128)(2,1)S(1)} %slice.34), channel_id=1, source_target_pairs={{0,96},{16,112},{1,97},{17,113},{2,98},{18,114},{3,99},{19,115},{4... | collective-permute-start | bytes 589832 | tf_op jit(solution)/shard_map/ppermute | solution.py:37
  47.8 6.4 %collective-permute-start.11 = (bf16[128,5632]{1,0:T(8,128)(2,1)}, bf16[128,5632]{1,0:T(8,128)(2,1)S(1)}, u32[]{:S(2)}, u32[]{:S(2)}) collective-permute-start(bf16[128,5632]{1,0:T(8,128)(2,1)} %collective-permute-done.10), channel_id=1, source_target_pairs={{0,16},{16,0},{1,17},{17,1},{2,18},{18,2},{3,19},{19,3},{4,20},{20... | collective-permute-start | bytes 4325384 | tf_op jit(solution)/shard_map/ppermute | solution.py:37
  58.8 2.6 %collective-permute-start.12 = (f32[1032,128]{1,0:T(8,128)S(1)}, f32[1032,128]{1,0:T(8,128)S(1)}, u32[]{:S(2)}, u32[]{:S(2)}) collective-permute-start(f32[1032,128]{1,0:T(8,128)S(1)} %get-tuple-element.37), channel_id=1, source_target_pairs={{0,16},{16,0},{1,17},{17,1},{2,18},{18,2},{3,19},{19,3},{4,20},{20... | collective-permute-start | bytes 1585160 | tf_op jit(solution)/shard_map/ppermute | solution.py:37
  61.7 7.7 %collective-permute-start.13 = (f16[1040,128]{1,0:T(8,128)(2,1)S(1)}, f16[1040,128]{1,0:T(8,128)(2,1)S(1)}, u32[]{:S(2)}, u32[]{:S(2)}) collective-permute-start(f16[1040,128]{1,0:T(8,128)(2,1)S(1)} %pad_maximum_fusion), channel_id=1, source_target_pairs={{0,8},{16,24},{1,9},{17,25},{2,10},{18,26},{3,11},{19,27},{4,12},{... | collective-permute-start | bytes 798728 | tf_op jit(solution)/shard_map/ppermute | solution.py:37
